TPU v7x, 32 devices: a whole 2x2x4 slice. The times are simulated.
32 devices in a mesh: dp: 8 (over y, x, core), narrow: 4 (over z).
Axes of the slice: x: 2, y: 2, z: 4, core: 2. Of those that a mesh axis runs over, the one named last changes fastest.
Arguments:
- tokens: bfloat16 [32768, 512], P(('dp', 'narrow')), may hold values from -6 to 6
- memory: bfloat16 [32, 512, 512], P(('dp', 'narrow')), may hold values from -6 to 6
- neighbour_bank: bfloat16 [32, 512, 512], P(('dp', 'narrow')), may hold values from -6 to 6
- starts: int32 [32768], P(('dp', 'narrow')), may hold values 0 or 1
- neighbours: int32 [32768, 4], P(('dp', 'narrow')), may hold values from 0 to 511
- cotangent: bfloat16 [32768, 512], P(('dp', 'narrow')), may hold values from -6 to 6
- attn_weights: float32 [4, 512, 512], P(None, 'dp', 'narrow'), may hold values from -0.375 to 0.375
- up_weights: float32 [512, 2048], P('dp', 'narrow'), may hold values from -0.25 to 0.25
- down_weights: float32 [2048, 512], P('narrow', 'dp'), may hold values from -0.125 to 0.125
- vectors: float32 [10, 512], replicated, as said below
- attn_moment: float32 [4, 512, 512], P(None, 'dp', 'narrow'), may hold values from -0.75 to 0.75
- up_moment: float32 [512, 2048], P('dp', 'narrow'), may hold values from -0.75 to 0.75
- down_moment: float32 [2048, 512], P('narrow', 'dp'), may hold values from -0.75 to 0.75
- vector_moment: float32 [10, 512], replicated, may hold values from -2 to 2
Outputs:
- out: bfloat16 [32768, 512], P(('dp', 'narrow'))
- grad_in: bfloat16 [32768, 512], P(('dp', 'narrow'))
- attn_new: float32 [4, 512, 512], P(None, 'dp', 'narrow')
- up_new: float32 [512, 2048], P('dp', 'narrow')
- down_new: float32 [2048, 512], P('narrow', 'dp')
- attn_mom_new: float32 [4, 512, 512], P(None, 'dp', 'narrow')
- up_mom_new: float32 [512, 2048], P('dp', 'narrow')
- down_mom_new: float32 [2048, 512], P('narrow', 'dp')
- vectors_new: float32 [10, 512], replicated
- vector_mom_new: float32 [10, 512], replicated
- grad_norm: float32 [], replicated
Inputs may be any that keep to these rules, and one draw needn't show every extreme that they name: `neighbours`: each entry names a row of the neighbour bank of the token's own segment. `starts`: 1 marks the first token of a document. `vectors`: rows 0 and 1 are positive norm gains, the other 8 rows the gate's weights.
All inputs are finite; a program needn't handle non-finite values. No bound on the sum of `starts` on one device may be relied on, other than what follows from the above.
Results may differ from a plain program's by a relative error of at most 0.022.
Values may be sent and summed in bfloat16 or wider, within the bound.
No kernel may reach another device: no remote copies, remote signals or barrier semaphores. Data moves between devices by JAX's collectives and lax.ppermute only.
A program may use at most 192 MiB of HBM per device.

v0:
```python
import math

import jax
import jax.numpy as jnp
from jax import lax
from jax.sharding import PartitionSpec as P

D = 512
H = 8
FF = 2048
MEM = 512
BANK = 512
KNB = 4
LEN = 1024
NS_ITERS = 5
PARAMS = 3150848


epsilon = 1e-06
coef_first = 3.4445
coef_second = -4.775
coef_third = 2.0315
clip_fraction = 0.05
muon_rate = 0.5
muon_decay = 0.5
vector_rate = 0.5
vector_decay = 0.9
masked_score = -1e30
highest = lax.Precision.HIGHEST
inverse_root_two = 0.7071067811865476
inverse_root_two_pi = 0.3989422804014327


def rms_factor(values):
    return lax.rsqrt(jnp.mean(values * values, axis=-1, keepdims=True) + epsilon)


def dot_plain(first_factor, second_factor):
    return jnp.dot(first_factor, second_factor, preferred_element_type=jnp.float32)


def dot_last(first_factor, second_factor):
    return lax.dot_general(
        first_factor, second_factor, (((1,), (1,)), ((), ())), preferred_element_type=jnp.float32
    )


def dot_first(first_factor, second_factor):
    return lax.dot_general(
        first_factor, second_factor, (((0,), (0,)), ((), ())), preferred_element_type=jnp.float32
    )


def to_pairs(matrix):
    row_count = matrix.shape[0]
    pair_size = min(2, H)
    return jnp.transpose(matrix.reshape(row_count, H // pair_size, pair_size, D // H), (1, 0, 2, 3))


def from_pairs(stacked):
    return jnp.transpose(stacked, (1, 0, 2, 3)).reshape(stacked.shape[1], D)


def visibility(seg_starts):
    doc_index = jnp.cumsum(seg_starts)
    before_reset = doc_index == 0
    positions = jnp.arange(LEN)
    causal = (positions[None, :] <= positions[:, None]) & (doc_index[None, :] == doc_index[:, None])
    return jnp.concatenate([jnp.broadcast_to(before_reset[:, None], (LEN, MEM)), causal], axis=1)


def masked_scores(query_pair, key_pair, visible_block):
    raw_scores = jnp.einsum(
        "rhd,chd->hrc", query_pair, key_pair, preferred_element_type=jnp.float32
    ) * (1.0 / math.sqrt(D // H))
    return jnp.where(visible_block[None], raw_scores, masked_score)


def segment_forward(full_weights, vectors, seg_tokens, seg_memory, seg_bank, seg_starts, seg_near):
    attn_full, up_full, down_full = full_weights
    head_dim = D // H
    score_scale = 1.0 / math.sqrt(head_dim)
    tokens_wide = seg_tokens.astype(jnp.float32)
    context = jnp.concatenate([seg_memory.astype(jnp.float32), tokens_wide], axis=0)
    normed = (context * rms_factor(context) * vectors[0]).astype(jnp.bfloat16)
    queries = dot_plain(normed[MEM:], attn_full[0]).astype(jnp.bfloat16)
    key_rows = dot_plain(normed, attn_full[1]).astype(jnp.bfloat16)
    value_rows = dot_plain(normed, attn_full[2]).astype(jnp.bfloat16)
    bank_keys = dot_plain(seg_bank, attn_full[1]).astype(jnp.bfloat16)
    bank_values = dot_plain(seg_bank, attn_full[2]).astype(jnp.bfloat16)
    visible = visibility(seg_starts)
    query_pairs = to_pairs(queries)
    key_pairs = to_pairs(key_rows)
    value_pairs = to_pairs(value_rows)
    block_rows = min(512, LEN)
    local_parts = []
    peak_parts = []
    total_parts = []
    for block_start in range(0, LEN, block_rows):
        visible_block = visible[block_start : block_start + block_rows]

        def pair_forward(operands):
            query_pair, key_pair, value_pair = operands
            scores = masked_scores(query_pair, key_pair, visible_block)
            row_peak = jnp.max(scores, axis=-1, keepdims=True)
            weights = jnp.exp(scores - row_peak)
            row_total = jnp.sum(weights, axis=-1, keepdims=True)
            probabilities = (weights / row_total).astype(jnp.bfloat16)
            result = jnp.einsum(
                "hrc,chd->rhd", probabilities, value_pair, preferred_element_type=jnp.float32
            )
            return (result, row_peak, row_total)

        results, block_peaks, block_totals = lax.map(
            pair_forward,
            (query_pairs[:, block_start : block_start + block_rows], key_pairs, value_pairs),
        )
        local_parts.append(from_pairs(results))
        peak_parts.append(block_peaks)
        total_parts.append(block_totals)
    local_out = jnp.concatenate(local_parts, axis=0)
    row_peaks = jnp.concatenate(peak_parts, axis=2)
    row_totals = jnp.concatenate(total_parts, axis=2)
    query_heads = queries.reshape(LEN, H, head_dim)
    near_keys = jnp.take(bank_keys, seg_near, axis=0).reshape(LEN, KNB, H, head_dim)
    near_values = jnp.take(bank_values, seg_near, axis=0).reshape(LEN, KNB, H, head_dim)
    near_scores = (
        jnp.einsum("qhd,qjhd->qjh", query_heads, near_keys, preferred_element_type=jnp.float32)
        * score_scale
    )
    near_peak = jnp.max(near_scores, axis=1, keepdims=True)
    near_weights = jnp.exp(near_scores - near_peak)
    near_probs = near_weights / jnp.sum(near_weights, axis=1, keepdims=True)
    fetched = jnp.sum(near_probs[..., None] * near_values, axis=1)
    gate_low = vectors[2:].astype(jnp.bfloat16)
    gate_open = jax.nn.sigmoid(dot_last(normed[MEM:], gate_low))
    gate_wide = gate_open[:, :, None]
    local_heads = local_out.reshape(LEN, H, head_dim)
    mixed_heads = (
        ((1.0 - gate_wide) * local_heads + gate_wide * fetched).reshape(LEN, D).astype(jnp.bfloat16)
    )
    residual = tokens_wide + dot_plain(mixed_heads, attn_full[3])
    ffn_in = (residual * rms_factor(residual) * vectors[1]).astype(jnp.bfloat16)
    hidden = dot_plain(ffn_in, up_full)
    activation = jax.nn.gelu(hidden, approximate=False).astype(jnp.bfloat16)
    output = residual + dot_plain(activation, down_full)
    saved = (
        normed,
        queries,
        key_rows,
        value_rows,
        bank_keys,
        bank_values,
        row_peaks,
        row_totals,
        local_out,
        near_probs,
        fetched,
        gate_open,
        mixed_heads,
        residual,
        ffn_in,
        hidden,
        activation,
    )
    return (output.astype(jnp.bfloat16), saved)


def segment_backward(
    full_weights, vectors, saved, seg_tokens, seg_memory, seg_bank, seg_starts, seg_near, seg_cot
):
    attn_full, up_full, down_full = full_weights
    (
        normed,
        queries,
        key_rows,
        value_rows,
        bank_keys,
        bank_values,
        row_peaks,
        row_totals,
        local_out,
        near_probs,
        fetched,
        gate_open,
        mixed_heads,
        residual,
        ffn_in,
        hidden,
        activation,
    ) = saved
    head_dim = D // H
    score_scale = 1.0 / math.sqrt(head_dim)
    grad_down = dot_first(activation, seg_cot)
    grad_activation = dot_last(seg_cot, down_full)
    gelu_slope = (
        0.5 * (1.0 + lax.erf(hidden * inverse_root_two))
        + hidden * jnp.exp(-0.5 * hidden * hidden) * inverse_root_two_pi
    )
    grad_hidden = (grad_activation * gelu_slope).astype(jnp.bfloat16)
    grad_up = dot_first(ffn_in, grad_hidden)
    grad_ffn_in = dot_last(grad_hidden, up_full)
    factor_ffn = rms_factor(residual)
    residual_hat = residual * factor_ffn
    grad_gain_ffn = jnp.sum(grad_ffn_in * residual_hat, axis=0)
    scaled_ffn = grad_ffn_in * vectors[1]
    grad_residual = seg_cot.astype(jnp.float32) + factor_ffn * (
        scaled_ffn - residual_hat * jnp.mean(scaled_ffn * residual_hat, axis=-1, keepdims=True)
    )
    branch_grad = grad_residual.astype(jnp.bfloat16)
    grad_out_weight = dot_first(mixed_heads, branch_grad)
    grad_mixed = dot_last(branch_grad, attn_full[3]).reshape(LEN, H, head_dim)
    local_heads = local_out.reshape(LEN, H, head_dim)
    gate_wide = gate_open[:, :, None]
    grad_gate = jnp.sum(grad_mixed * (fetched - local_heads), axis=-1)
    grad_logits = (grad_gate * gate_open * (1.0 - gate_open)).astype(jnp.bfloat16)
    grad_local = (grad_mixed * (1.0 - gate_wide)).reshape(LEN, D).astype(jnp.bfloat16)
    grad_fetched = grad_mixed * gate_wide
    query_heads = queries.reshape(LEN, H, head_dim)
    near_keys = jnp.take(bank_keys, seg_near, axis=0).reshape(LEN, KNB, H, head_dim)
    near_values = jnp.take(bank_values, seg_near, axis=0).reshape(LEN, KNB, H, head_dim)
    grad_near_probs = jnp.sum(grad_fetched[:, None] * near_values, axis=-1)
    grad_near_values = near_probs[..., None] * grad_fetched[:, None]
    weighted = jnp.sum(near_probs * grad_near_probs, axis=1, keepdims=True)
    grad_near_scores = near_probs * (grad_near_probs - weighted) * score_scale
    grad_query_near = jnp.sum(grad_near_scores[..., None] * near_keys, axis=1)
    grad_near_keys = grad_near_scores[..., None] * query_heads[:, None]
    flat_near = seg_near.reshape(-1)
    bank_grad_keys = jax.ops.segment_sum(
        grad_near_keys.reshape(LEN * KNB, D), flat_near, num_segments=BANK
    ).astype(jnp.bfloat16)
    bank_grad_values = jax.ops.segment_sum(
        grad_near_values.reshape(LEN * KNB, D), flat_near, num_segments=BANK
    ).astype(jnp.bfloat16)
    visible = visibility(seg_starts)
    query_pairs = to_pairs(queries)
    key_pairs = to_pairs(key_rows)
    value_pairs = to_pairs(value_rows)
    grad_local_pairs = to_pairs(grad_local)
    block_rows = min(512, LEN)
    query_parts = []
    grad_key_total = jnp.zeros(key_pairs.shape, jnp.float32)
    grad_value_total = jnp.zeros(value_pairs.shape, jnp.float32)
    for block_start in range(0, LEN, block_rows):
        visible_block = visible[block_start : block_start + block_rows]

        def pair_backward(operands):
            query_pair, key_pair, value_pair, grad_pair, row_peak, row_total = operands
            scores = masked_scores(query_pair, key_pair, visible_block)
            probabilities = jnp.exp(scores - row_peak) / row_total
            probs_low = probabilities.astype(jnp.bfloat16)
            grad_value_pair = jnp.einsum(
                "hrc,rhd->chd", probs_low, grad_pair, preferred_element_type=jnp.float32
            )
            grad_probs = jnp.einsum(
                "rhd,chd->hrc", grad_pair, value_pair, preferred_element_type=jnp.float32
            )
            row_dot = jnp.sum(probabilities * grad_probs, axis=-1, keepdims=True)
            grad_scores = (probabilities * (grad_probs - row_dot)).astype(jnp.bfloat16)
            grad_query_pair = (
                jnp.einsum(
                    "hrc,chd->rhd", grad_scores, key_pair, preferred_element_type=jnp.float32
                )
                * score_scale
            )
            grad_key_pair = (
                jnp.einsum(
                    "hrc,rhd->chd", grad_scores, query_pair, preferred_element_type=jnp.float32
                )
                * score_scale
            )
            return (grad_query_pair, grad_key_pair, grad_value_pair)

        block_query, block_keys, block_values = lax.map(
            pair_backward,
            (
                query_pairs[:, block_start : block_start + block_rows],
                key_pairs,
                value_pairs,
                grad_local_pairs[:, block_start : block_start + block_rows],
                row_peaks[:, :, block_start : block_start + block_rows],
                row_totals[:, :, block_start : block_start + block_rows],
            ),
        )
        query_parts.append(from_pairs(block_query))
        grad_key_total = grad_key_total + block_keys
        grad_value_total = grad_value_total + block_values
    grad_query = (jnp.concatenate(query_parts, axis=0) + grad_query_near.reshape(LEN, D)).astype(
        jnp.bfloat16
    )
    grad_keys_low = from_pairs(grad_key_total).astype(jnp.bfloat16)
    grad_values_low = from_pairs(grad_value_total).astype(jnp.bfloat16)
    grad_query_weight = dot_first(normed[MEM:], grad_query)
    grad_key_weight = dot_first(normed, grad_keys_low) + dot_first(seg_bank, bank_grad_keys)
    grad_value_weight = dot_first(normed, grad_values_low) + dot_first(seg_bank, bank_grad_values)
    gate_low = vectors[2:].astype(jnp.bfloat16)
    grad_gate_rows = dot_first(grad_logits, normed[MEM:])
    grad_normed = dot_last(grad_keys_low, attn_full[1]) + dot_last(grad_values_low, attn_full[2])
    grad_normed_tokens = dot_last(grad_query, attn_full[0]) + dot_plain(grad_logits, gate_low)
    grad_normed = jnp.concatenate(
        [grad_normed[:MEM], grad_normed[MEM:] + grad_normed_tokens], axis=0
    )
    context = jnp.concatenate(
        [seg_memory.astype(jnp.float32), seg_tokens.astype(jnp.float32)], axis=0
    )
    factor_attn = rms_factor(context)
    context_hat = context * factor_attn
    grad_gain_attn = jnp.sum(grad_normed * context_hat, axis=0)
    scaled_attn = grad_normed[MEM:] * vectors[0]
    hat_tokens = context_hat[MEM:]
    grad_tokens = grad_residual + factor_attn[MEM:] * (
        scaled_attn - hat_tokens * jnp.mean(scaled_attn * hat_tokens, axis=-1, keepdims=True)
    )
    grad_attn = jnp.stack([grad_query_weight, grad_key_weight, grad_value_weight, grad_out_weight])
    grad_vectors = jnp.concatenate(
        [grad_gain_attn[None], grad_gain_ffn[None], grad_gate_rows], axis=0
    )
    return ((grad_attn, grad_up, grad_down, grad_vectors), grad_tokens.astype(jnp.bfloat16))


def per_device(
    tokens,
    memory,
    neighbour_bank,
    starts,
    neighbours,
    cotangent,
    attn_weights,
    up_weights,
    down_weights,
    vectors,
    attn_moment,
    up_moment,
    down_moment,
    vector_moment,
):
    segments = tokens.shape[0] // LEN
    attn_low = attn_weights.astype(jnp.bfloat16)
    up_low = up_weights.astype(jnp.bfloat16)
    down_low = down_weights.astype(jnp.bfloat16)
    rows_attn, rows_up, rows_down = (
        lax.all_gather(attn_low, "dp", axis=1, tiled=True),
        lax.all_gather(up_low, "dp", axis=0, tiled=True),
        lax.all_gather(down_low, "dp", axis=1, tiled=True),
    )
    forward_full = (
        lax.all_gather(rows_attn, "narrow", axis=2, tiled=True),
        lax.all_gather(rows_up, "narrow", axis=1, tiled=True),
        lax.all_gather(rows_down, "narrow", axis=0, tiled=True),
    )
    segment_inputs = (
        tokens.reshape(segments, LEN, D),
        memory,
        neighbour_bank,
        starts.reshape(segments, LEN),
        neighbours.reshape(segments, LEN, KNB),
    )

    def forward_step(scan_carry, scan_items):
        seg_tokens, seg_memory, seg_bank, seg_starts, seg_near = scan_items
        output, saved = segment_forward(
            forward_full, vectors, seg_tokens, seg_memory, seg_bank, seg_starts, seg_near
        )
        return (scan_carry, (output, saved))

    scan_end, (outputs, saved_all) = lax.scan(
        forward_step, jnp.zeros((), jnp.float32), segment_inputs
    )
    back_attn, back_up, back_down = (
        lax.all_gather(attn_low, "dp", axis=1, tiled=True),
        lax.all_gather(up_low, "dp", axis=0, tiled=True),
        lax.all_gather(down_low, "dp", axis=1, tiled=True),
    )
    backward_full = (
        lax.all_gather(back_attn, "narrow", axis=2, tiled=True),
        lax.all_gather(back_up, "narrow", axis=1, tiled=True),
        lax.all_gather(back_down, "narrow", axis=0, tiled=True),
    )

    def backward_step(totals, scan_items):
        saved_one, seg_tokens, seg_memory, seg_bank, seg_starts, seg_near, seg_cot = scan_items
        seg_grads, grad_tokens = segment_backward(
            backward_full,
            vectors,
            saved_one,
            seg_tokens,
            seg_memory,
            seg_bank,
            seg_starts,
            seg_near,
            seg_cot,
        )
        return (jax.tree.map(jnp.add, totals, seg_grads), grad_tokens)

    zero_grads = (
        jnp.zeros((4, D, D), jnp.float32),
        jnp.zeros((D, FF), jnp.float32),
        jnp.zeros((FF, D), jnp.float32),
        jnp.zeros(vectors.shape, jnp.float32),
    )
    totals, grad_in = lax.scan(
        backward_step,
        zero_grads,
        (saved_all,) + segment_inputs + (cotangent.reshape(segments, LEN, D),),
    )
    grad_attn, grad_up, grad_down, grad_vectors = totals
    narrow_attn, narrow_up, narrow_down = (
        lax.psum_scatter(
            grad_attn.astype(jnp.bfloat16), "narrow", scatter_dimension=2, tiled=True
        ).astype(jnp.float32),
        lax.psum_scatter(
            grad_up.astype(jnp.bfloat16), "narrow", scatter_dimension=1, tiled=True
        ).astype(jnp.float32),
        lax.psum_scatter(
            grad_down.astype(jnp.bfloat16), "narrow", scatter_dimension=0, tiled=True
        ).astype(jnp.float32),
    )
    clip_limit = clip_fraction * math.sqrt(PARAMS)
    dp_index = lax.axis_index("dp")
    row_share = D // lax.axis_size("dp")
    row_start = dp_index * row_share
    owned_attn, owned_up, owned_down = (
        lax.psum_scatter(
            narrow_attn.astype(jnp.bfloat16), "dp", scatter_dimension=1, tiled=True
        ).astype(jnp.float32),
        lax.psum_scatter(
            narrow_up.astype(jnp.bfloat16), "dp", scatter_dimension=0, tiled=True
        ).astype(jnp.float32),
        lax.psum_scatter(
            narrow_down.astype(jnp.bfloat16), "dp", scatter_dimension=1, tiled=True
        ).astype(jnp.float32),
    )
    own_squares = (
        jnp.sum(owned_attn * owned_attn)
        + jnp.sum(owned_up * owned_up)
        + jnp.sum(owned_down * owned_down)
    )
    vector_sum, square_sum = lax.psum((grad_vectors, own_squares), ("dp", "narrow"))
    grad_norm = jnp.sqrt(square_sum + jnp.sum(vector_sum * vector_sum))
    clip_factor = clip_limit / jnp.maximum(grad_norm, clip_limit)
    attn_mom_new = muon_decay * attn_moment + clip_factor * owned_attn
    up_mom_new = muon_decay * up_moment + clip_factor * owned_up
    down_mom_new = muon_decay * down_moment + clip_factor * owned_down
    ortho_attn, ortho_up, ortho_down = (
        lax.all_gather(attn_mom_new.astype(jnp.bfloat16), "dp", axis=1, tiled=True).astype(
            attn_mom_new.dtype
        ),
        lax.all_gather(up_mom_new.astype(jnp.bfloat16), "dp", axis=0, tiled=True).astype(
            up_mom_new.dtype
        ),
        lax.all_gather(down_mom_new.astype(jnp.bfloat16), "dp", axis=1, tiled=True).astype(
            down_mom_new.dtype
        ),
    )
    for iteration in range(NS_ITERS):
        gram_attn = jnp.einsum("imc,inc->imn", ortho_attn, ortho_attn, precision=highest)
        gram_up = lax.dot_general(ortho_up, ortho_up, (((1,), (1,)), ((), ())), precision=highest)
        gram_down = lax.dot_general(
            ortho_down, ortho_down, (((0,), (0,)), ((), ())), precision=highest
        )
        partial_grams = jnp.concatenate([gram_attn, gram_up[None], gram_down[None]], axis=0)
        gram_total = lax.psum(partial_grams.astype(jnp.bfloat16), "narrow").astype(jnp.float32)
        if iteration == 0:
            norm_scales = 1.0 / (jnp.sqrt(jnp.trace(gram_total, axis1=1, axis2=2)) + 1e-07)
            ortho_attn = ortho_attn * norm_scales[:4, None, None]
            ortho_up = ortho_up * norm_scales[4]
            ortho_down = ortho_down * norm_scales[5]
            gram_total = gram_total * (norm_scales * norm_scales)[:, None, None]
        once_attn = jnp.einsum("imn,inc->imc", gram_total[:4], ortho_attn, precision=highest)
        twice_attn = jnp.einsum("imn,inc->imc", gram_total[:4], once_attn, precision=highest)
        ortho_attn = coef_first * ortho_attn + coef_second * once_attn + coef_third * twice_attn
        once_up = jnp.dot(gram_total[4], ortho_up, precision=highest)
        twice_up = jnp.dot(gram_total[4], once_up, precision=highest)
        ortho_up = coef_first * ortho_up + coef_second * once_up + coef_third * twice_up
        once_down = jnp.dot(ortho_down, gram_total[5], precision=highest)
        twice_down = jnp.dot(once_down, gram_total[5], precision=highest)
        ortho_down = coef_first * ortho_down + coef_second * once_down + coef_third * twice_down
    final_attn = lax.dynamic_slice_in_dim(ortho_attn, row_start, row_share, 1)
    final_up = lax.dynamic_slice_in_dim(ortho_up, row_start, row_share, 0)
    final_down = lax.dynamic_slice_in_dim(ortho_down, row_start, row_share, 1)
    shape_factor = math.sqrt(max(1.0, FF / D))
    attn_new = attn_weights - muon_rate * final_attn
    up_new = up_weights - muon_rate * final_up
    down_new = down_weights - muon_rate * shape_factor * final_down
    vector_mom_new = vector_decay * vector_moment + clip_factor * vector_sum
    vectors_new = vectors - vector_rate * vector_mom_new
    return (
        outputs.reshape(segments * LEN, D),
        grad_in.reshape(segments * LEN, D),
        attn_new,
        up_new,
        down_new,
        attn_mom_new,
        up_mom_new,
        down_mom_new,
        vectors_new,
        vector_mom_new,
        grad_norm,
    )


def solution(mesh):
    placed = (
        P(("dp", "narrow"), None),
        P(("dp", "narrow"), None, None),
        P(("dp", "narrow"), None, None),
        P(("dp", "narrow")),
        P(("dp", "narrow"), None),
        P(("dp", "narrow"), None),
        P(None, "dp", "narrow"),
        P("dp", "narrow"),
        P("narrow", "dp"),
        P(),
        P(None, "dp", "narrow"),
        P("dp", "narrow"),
        P("narrow", "dp"),
        P(),
    )
    return jax.shard_map(
        per_device,
        mesh=mesh,
        in_specs=placed,
        out_specs=(
            P(("dp", "narrow"), None),
            P(("dp", "narrow"), None),
            P(None, "dp", "narrow"),
            P("dp", "narrow"),
            P("narrow", "dp"),
            P(None, "dp", "narrow"),
            P("dp", "narrow"),
            P("narrow", "dp"),
            P(),
            P(),
            P(),
        ),
        check_vma=False,
    )
```

profile of v0, /device:TPU:0, one launch (start us, length us, event | category | flops | bytes accessed | tf_op | source)
XLA Modules:
  0.0 1541.1 jit_solution(4447016412917603916)
XLA Ops:
  8.3 12.4 all_gather.33
  21.7 10.7 all_gather.35
  33.4 9.9 all_gather.37
  56.8 10.6 all-gather.4.cloned.1.call-done
  77.6 32.5 %while.76 = (s32[]{:T(128)}, f32[4,512,2,64]{1,3,2,0:T(8,128)}, f32[4,2,512,1]{2,1,3,0:T(2,128)S(1)}, f32[4,2,512,1]{2,1,3,0:T(2,128)S(1)}, bf16[4,1536,2,64]{1,...) while((s32[]{:T(128)}, f32[4,512,2,64]{1,3,2,0:T(8,128)}, ...), condition=%wide.region_6.7_spmd, body=%wide.region_3.6_spmd.sunk | while | flops 421525504 | bytes 22452328 | solution.py:114
  111.4 32.6 %while.106 = (s32[]{:T(128)}, f32[4,512,2,64]{1,3,2,0:T(8,128)}, f32[4,2,512,1]{2,1,3,0:T(2,128)S(1)}, f32[4,2,512,1]{2,1,3,0:T(2,128)S(1)}, bf16[4,1536,2,64]{1...) while((s32[]{:T(128)}, f32[4,512,2,64]{1,3,2,0:T(8,128)}, ...), condition=%wide.region_10.11_spmd, body=%wide.region_7.10_spmd.sunk | while | flops 421525504 | bytes 22452328 | solution.py:114
  145.4 17.7 %gather_fusion.1 = bf16[4096,512]{1,0:T(8,128)(2,1)} fusion(bf16[512,512]{1,0:T(8,128)(2,1)S(1)} %convolution_convert_fusion.12, s32[4096]{0:T(1024)S(1)} %broadcast_clamp_fusion), kind=kCustom, calls=%fused_computation.1.clone | custom fusion | bytes 8404992 | tf_op jit(solution)/shard_map/while/body/eval_jaxpr/jit(_take)/gather | solution.py:126
  163.2 6.9 reshape.436
  170.1 7.5 copy.99
  179.1 17.3 %gather_fusion = bf16[4096,512]{1,0:T(8,128)(2,1)} fusion(bf16[512,512]{1,0:T(8,128)(2,1)S(1)} %convolution_convert_fusion.13, s32[4096]{0:T(1024)S(1)} %broadcast_clamp_fusion), kind=kCustom, calls=%fused_computation.clone | custom fusion | bytes 8404992 | tf_op jit(solution)/shard_map/while/body/eval_jaxpr/jit(_take)/gather | solution.py:125
  196.4 6.9 reshape.432
  203.3 7.6 copy.97
  222.7 23.1 %fusion.98 = (bf16[1024,2048]{1,0:T(8,128)(2,1)S(1)}, f32[1024,2048]{1,0:T(8,128)}) fusion(bf16[512,2048]{1,0:T(8,128)(2,1)} %all-gather.6.cloned.1.call-done, f32[1024,512]{0,1:T(8,128)} %get-tuple-element.576, f32[512]{0:T(512)S(1)} %bitcast.543, f32[1024]{0:T(1024)S(1)} %add_rsqrt_fusion.1), kind=kOutput, calls=%fused_computation.120 | convolution fusion | flops 2285371392 | bytes 16783360 | tf_op jit(solution)/shard_map/while/body/eval_jaxpr/dot_general | solution.py:39
  251.8 7.5 fusion.104
  273.8 53.3 %while.108 = (s32[]{:T(128)}, f32[4,512,2,64]{1,3,2,0:T(8,128)}, f32[4,1536,2,64]{1,3,2,0:T(8,128)}, f32[4,1536,2,64]{1,3,2,0:T(8,128)}, bf16[4,1536,2,64]{1,3,2...) while((s32[]{:T(128)}, f32[4,512,2,64]{1,3,2,0:T(8,128)}, ...), condition=%wide.region_21.23_spmd, body=%wide.region_19.22_spmd.sunk | while | flops 1022622720 | bytes 51549312 | solution.py:274
  327.2 6.5 convolution_convert_fusion.1
  339.1 56.1 %while.107 = (s32[]{:T(128)}, f32[4,512,2,64]{1,3,2,0:T(8,128)}, f32[4,1536,2,64]{1,3,2,0:T(8,128)}, f32[4,1536,2,64]{1,3,2,0:T(8,128)}, bf16[4,1536,2,64]{1,3,2...) while((s32[]{:T(128)}, f32[4,512,2,64]{1,3,2,0:T(8,128)}, ...), condition=%wide.region_18.20_spmd, body=%wide.region_16.19_spmd.sunk | while | flops 1022622720 | bytes 51549312 | solution.py:274
  369.8 3.9 multiply_reduce_fusion.14
  395.2 8.0 broadcast_multiply_fusion.1
  405.8 4.3 broadcast_multiply_fusion
  410.2 16.2 %copy.109 = f32[1024,4,8,64]{3,2,1,0:T(8,128)} copy(f32[1024,4,8,64]{0,3,2,1:T(8,128)} %broadcast_multiply_fusion) | data formatting | bytes 16777216 | tf_op jit(solution)/shard_map/while/body/eval_jaxpr/mul | solution.py:227
  426.4 14.2 reshape.411
  440.6 16.6 %copy.111 = f32[1024,4,8,64]{3,2,1,0:T(8,128)} copy(f32[1024,4,8,64]{0,3,2,1:T(8,128)} %get-tuple-element.556) | data formatting | bytes 16777216 | tf_op jit(solution)/shard_map/while/body/eval_jaxpr/mul | solution.py:223
  457.1 14.4 reshape.419
  474.7 25.4 %scatter_custom_fusion = f32[512,512]{1,0:T(8,128)S(1)} fusion(s32[4096]{0:T(1024)} %reshape.409, f32[4096,512]{1,0:T(8,128)} %reshape.411, f32[]{:T(128)} %constant.329.clone.1), kind=kCustom, calls=%fused_computation.309 | custom fusion | flops 2097152 | bytes 1049088 | tf_op jit(solution)/shard_map/while/body/eval_jaxpr/scatter-add | solution.py:229
  500.1 25.6 %scatter_custom_fusion.1 = f32[512,512]{1,0:T(8,128)S(1)} fusion(s32[4096]{0:T(1024)} %reshape.409, f32[4096,512]{1,0:T(8,128)} %reshape.419, f32[]{:T(128)} %constant.329.clone.1), kind=kCustom, calls=%fused_computation.307 | custom fusion | flops 2097152 | bytes 1049088 | tf_op jit(solution)/shard_map/while/body/eval_jaxpr/scatter-add | solution.py:232
  525.8 5.8 add_convert_fusion
  540.8 4.5 copy.153
  559.8 4.1 multiply_reduce_fusion.6
  563.8 27.3 %reduce-scatter.19.cloned.1.call-done = bf16[128,2048]{1,0:T(8,128)(2,1)} async-done(((bf16[512,2048]{1,0:T(8,128)(2,1)}), bf16[128,2048]{1,0:T(8,128)(2,1)}) %reduce-scatter.19.cloned.1.call-update) | async-done | bytes 524304
  598.7 29.3 %reduce-scatter.21.cloned.1.call-done = bf16[64,512]{1,0:T(8,128)(2,1)} async-done(((bf16[512,512]{1,0:T(8,128)(2,1)}), bf16[64,512]{1,0:T(8,128)(2,1)}) %reduce-scatter.21.cloned.1.call-update) | async-done | bytes 65552
  629.0 36.3 %reduce-scatter.15.cloned.1.call-done = bf16[64,512]{1,0:T(8,128)(2,1)} async-done(((bf16[512,512]{1,0:T(8,128)(2,1)}), bf16[64,512]{1,0:T(8,128)(2,1)}) %reduce-scatter.15.cloned.1.call-update) | async-done | bytes 65552 | tf_op jit(solution)/shard_map/reduce_scatter | solution.py:426
  667.4 36.0 %reduce-scatter.11.cloned.1.call-done = bf16[4,64,128]{2,1,0:T(8,128)(2,1)} async-done(((bf16[4,512,128]{2,1,0:T(8,128)(2,1)}), bf16[4,64,128]{2,1,0:T(8,128)(2,1)}) %reduce-scatter.11.cloned.1.call-update) | async-done | bytes 65552 | tf_op jit(solution)/shard_map/reduce_scatter | solution.py:423
  707.0 39.8 %all-reduce = (f32[]{:T(128)}, f32[10,512]{1,0:T(8,128)S(1)}) all-reduce(f32[]{:T(128)S(6)} %add.308, f32[10,512]{1,0:T(8,128)S(1)} %pad_maximum_fusion.8), channel_id=1, replica_groups=mesh['dp'=8,'narrow'=4] {'dp','narrow'}, use_global_device_ids=true, to_apply=%region_38.40 | all-reduce | flops 5121 | bytes 40968 | tf_op jit(solution)/shard_map/psum | solution.py:438
  751.1 11.0 all_gather.39
  763.9 9.8 all_gather.40
  773.8 8.9 all_gather.41
  788.9 118.1 %all-reduce.7.cloned.1.call-done = bf16[6,512,512]{2,1,0:T(8,128)(2,1)} async-done(((bf16[6,512,512]{2,1,0:T(8,128)(2,1)}), bf16[6,512,512]{2,1,0:T(8,128)(2,1)}) %all-reduce.7.cloned.1.call-update) | async-done | bytes 3145744 | tf_op jit(solution)/shard_map/psum | solution.py:462
  910.7 5.1 fusion.159
  915.9 4.0 fusion.132
  920.9 4.7 convolution_convert_fusion.7
  935.4 4.6 fusion.128
  945.7 4.0 fusion.129
  955.1 120.2 %all-reduce.9.cloned.1.call-done = bf16[6,512,512]{2,1,0:T(8,128)(2,1)} async-done(((bf16[6,512,512]{2,1,0:T(8,128)(2,1)}), bf16[6,512,512]{2,1,0:T(8,128)(2,1)}) %all-reduce.9.cloned.1.call-update) | async-done | bytes 3145744 | tf_op jit(solution)/shard_map/psum | solution.py:462
  1102.3 120.2 %all-reduce.11.cloned.1.call-done = bf16[6,512,512]{2,1,0:T(8,128)(2,1)} async-done(((bf16[6,512,512]{2,1,0:T(8,128)(2,1)}), bf16[6,512,512]{2,1,0:T(8,128)(2,1)}) %all-reduce.11.cloned.1.call-update) | async-done | bytes 3145744 | tf_op jit(solution)/shard_map/psum | solution.py:462
  1249.7 120.2 %all-reduce.13.cloned.1.call-done = bf16[6,512,512]{2,1,0:T(8,128)(2,1)} async-done(((bf16[6,512,512]{2,1,0:T(8,128)(2,1)}), bf16[6,512,512]{2,1,0:T(8,128)(2,1)}) %all-reduce.13.cloned.1.call-update) | async-done | bytes 3145744 | tf_op jit(solution)/shard_map/psum | solution.py:462
  1397.8 6.8 add_convert_fusion.3
  1414.4 102.7 %all-reduce.15.cloned.1.call-done = bf16[6,512,512]{2,1,0:T(8,128)(2,1)} async-done(((bf16[6,512,512]{2,1,0:T(8,128)(2,1)}), bf16[6,512,512]{2,1,0:T(8,128)(2,1)}) %all-reduce.15.cloned.1.call-update) | async-done | bytes 3145744 | tf_op jit(solution)/shard_map/psum | solution.py:462
  (502 shorter events, 423.7 us)
Async XLA Ops:
  7.2 136.8 %copy-start = (bf16[1,512,512]{2,1,0:T(8,128)(2,1)S(1)}, bf16[1,512,512]{2,1,0:T(8,128)(2,1)}, u32[]{:S(2)}) copy-start(bf16[1,512,512]{2,1,0:T(8,128)(2,1)} %param.26) | copy-start | bytes 1572868
  7.2 36.2 %copy-start.88 = (s32[1024,4]{0,1:T(4,128)S(1)}, s32[1024,4]{0,1:T(4,128)}, u32[]{:S(2)}) copy-start(s32[1024,4]{0,1:T(4,128)} %param.28) | copy-start | bytes 49156
  7.2 37.1 %copy-start.104 = (s32[1024]{0:T(1024)S(1)}, s32[1024]{0:T(1024)}, u32[]{:S(2)}) copy-start(s32[1024]{0:T(1024)} %param.27) | copy-start | bytes 12292
  7.2 37.7 %copy-start.94 = (f32[10,512]{1,0:T(8,128)S(1)}, f32[10,512]{1,0:T(8,128)}, u32[]{:S(2)}) copy-start(f32[10,512]{1,0:T(8,128)} %param.33) | copy-start | bytes 61444
  7.2 38.8 %copy-start.83 = (bf16[1,512,512]{2,1,0:T(8,128)(2,1)S(1)}, bf16[1,512,512]{2,1,0:T(8,128)(2,1)}, u32[]{:S(2)}) copy-start(bf16[1,512,512]{2,1,0:T(8,128)(2,1)} %param.25) | copy-start | bytes 1572868
  7.2 60.2 %all-gather.4.cloned.1.call-start = ((), (), s32[]{:S(2)}) async-start(), calls=%async_computation.6 | async-start | bytes 2621440 | tf_op jit(solution)/shard_map/all_gather | solution.py:347
  20.7 202.0 %all-gather.6.cloned.1.call-start = ((), (), s32[]{:S(2)}) async-start(), calls=%async_computation.7 | async-start | bytes 2621440 | tf_op jit(solution)/shard_map/all_gather | solution.py:348
  32.4 219.3 %all-gather.8.cloned.1.call-start = ((), (), s32[]{:S(2)}) async-start(), calls=%async_computation.8 | async-start | bytes 2621440 | tf_op jit(solution)/shard_map/all_gather | solution.py:349
  43.4 505.6 %reduce-scatter.17.cloned.1.call-start = ((), (), s32[]{:S(2)}) async-start(), calls=%async_computation.12 | async-start | bytes 2621440 | tf_op jit(solution)/shard_map/reduce_scatter | solution.py:414
  45.5 7.8 copy-start.100
  203.3 7.6 copy-start.29
  203.3 7.6 copy-start.92
  211.0 5.7 copy-start.8
  217.8 45.3 %copy-start.5 = (f32[1024,512]{0,1:T(8,128)}, f32[1024,512]{0,1:T(8,128)S(1)}, u32[]{:S(2)}) copy-start(f32[1024,512]{0,1:T(8,128)S(1)} %fusion.106) | copy-start | bytes 6291460
  222.7 25.2 %copy-start.78 = (bf16[1024,512]{1,0:T(8,128)(2,1)S(1)}, bf16[1024,512]{1,0:T(8,128)(2,1)}, u32[]{:S(2)}) copy-start(bf16[1024,512]{1,0:T(8,128)(2,1)} %param.29) | copy-start | bytes 3145732
  251.7 305.1 %reduce-scatter.13.cloned.1.call-start = ((), (), s32[]{:S(2)}) async-start(), calls=%async_computation.10 | async-start | bytes 2621440 | tf_op jit(solution)/shard_map/reduce_scatter | solution.py:411
  251.7 7.5 copy-start.71
  251.7 7.5 copy-start.106
  333.7 257.4 %reduce-scatter.19.cloned.1.call-start = ((), (), s32[]{:S(2)}) async-start(), calls=%async_computation.18 | async-start | bytes 2621440
  339.1 56.1 %copy-start.75 = (f32[1024,4,8]{0,2,1:T(8,128)S(1)}, f32[1024,4,8]{0,2,1:T(8,128)}, u32[]{:S(2)}) copy-start(f32[1024,4,8]{0,2,1:T(8,128)} %copy-done.74) | copy-start | bytes 393220
  339.1 56.1 %copy-start.93 = (pred[1024,4]{0,1:T(4,128)(4,1)S(1)}, pred[1024,4]{0,1:T(4,128)(4,1)}, u32[]{:S(2)}) copy-start(pred[1024,4]{0,1:T(4,128)(4,1)} %compare_and_fusion) | copy-start | bytes 12292
  395.2 8.0 copy-start.58
  395.2 8.0 copy-start.81
  395.2 8.0 copy-start.87
  395.2 8.1 copy-start.7
  457.1 14.4 copy-start.6
  457.1 14.4 copy-start.73
  457.1 14.4 copy-start.77
  525.7 5.8 copy-start.45
  548.9 79.2 %reduce-scatter.21.cloned.1.call-start = ((), (), s32[]{:S(2)}) async-start(), calls=%async_computation.19 | async-start | bytes 589824
  551.0 114.2 %reduce-scatter.15.cloned.1.call-start = ((), (), s32[]{:S(2)}) async-start(), calls=%async_computation.11 | async-start | bytes 589824 | tf_op jit(solution)/shard_map/reduce_scatter | solution.py:426
  556.8 146.7 %reduce-scatter.11.cloned.1.call-start = ((), (), s32[]{:S(2)}) async-start(), calls=%async_computation.9 | async-start | bytes 589824 | tf_op jit(solution)/shard_map/reduce_scatter | solution.py:423
  593.8 313.2 %all-reduce.7.cloned.1.call-start = ((), (), s32[]{:S(2)}) async-start(), calls=%async_computation.13 | async-start | bytes 6291456 | tf_op jit(solution)/shard_map/psum | solution.py:462
  595.5 111.4 %copy-start.90 = (f32[512,64]{0,1:T(8,128)S(1)}, f32[512,64]{0,1:T(8,128)}, u32[]{:S(2)}) copy-start(f32[512,64]{0,1:T(8,128)} %param.36) | copy-start | bytes 393220
  595.5 154.1 %copy-start.91 = (f32[4,64,128]{2,1,0:T(8,128)S(1)}, f32[4,64,128]{2,1,0:T(8,128)}, u32[]{:S(2)}) copy-start(f32[4,64,128]{2,1,0:T(8,128)} %param.34) | copy-start | bytes 393220
  762.1 21.8 %copy-start.54 = (bf16[4,512,128]{2,1,0:T(8,128)(2,1)}, bf16[4,512,128]{2,1,0:T(8,128)(2,1)S(1)}, u32[]{:S(2)}) copy-start(bf16[4,512,128]{2,1,0:T(8,128)(2,1)S(1)} %all_gather.39) | copy-start | bytes 1572868
  786.7 288.6 %all-reduce.9.cloned.1.call-start = ((), (), s32[]{:S(2)}) async-start(), calls=%async_computation.14 | async-start | bytes 6291456 | tf_op jit(solution)/shard_map/psum | solution.py:462
  939.9 9.7 copy-start.18
  945.7 7.3 copy-start.46
  955.0 267.4 %all-reduce.11.cloned.1.call-start = ((), (), s32[]{:S(2)}) async-start(), calls=%async_computation.15 | async-start | bytes 6291456 | tf_op jit(solution)/shard_map/psum | solution.py:462
  1081.2 5.2 copy-start.20
  1102.2 267.7 %all-reduce.13.cloned.1.call-start = ((), (), s32[]{:S(2)}) async-start(), calls=%async_computation.16 | async-start | bytes 6291456 | tf_op jit(solution)/shard_map/psum | solution.py:462
  1228.4 5.2 copy-start.15
  1249.6 267.4 %all-reduce.15.cloned.1.call-start = ((), (), s32[]{:S(2)}) async-start(), calls=%async_computation.17 | async-start | bytes 6291456 | tf_op jit(solution)/shard_map/psum | solution.py:462
  1406.9 6.1 copy-start.79
  1406.9 6.8 copy-start.102
  1410.6 106.5 %copy-start.28 = (f32[512,512]{1,0:T(8,128)S(1)}, f32[512,512]{1,0:T(8,128)}, u32[]{:S(2)}) copy-start(f32[512,512]{1,0:T(8,128)} %copy-done.27) | copy-start | bytes 3145732
  1523.0 5.9 copy-start.34
  (76 other events, 191.8 us)
Sparse Core Ops, SparseCore 0:
  20.8 46.5 all-gather.3
  69.0 44.1 all-gather.5
  114.8 44.6 all-gather.7
  251.8 42.1 reduce-scatter.16
  333.9 42.0 reduce-scatter.12
  549.0 42.1 reduce-scatter.18
  594.6 33.4 reduce-scatter.20
  631.1 34.1 reduce-scatter.14
  669.2 34.1 reduce-scatter.10
  786.8 120.1 all-reduce.6
  955.2 120.0 all-reduce.8
  1102.3 120.0 all-reduce.10
  1249.7 120.0 all-reduce.12
  1396.9 120.0 all-reduce.14
where the time goes:
time: 1550 us; the launch traced here: 1540 us
  waiting for transfers between devices  721 us (47%)
  matrix products  344 us (22%)
  local copies, waits for them, and re-layouts  209 us (13%)
  other arithmetic  143 us (9%)
  blocking collectives  103 us (7%)
  between operations  20.2 us (1%)
    psum x5, waiting for transfers between devices, per_device(): lax.psum(partial_grams.astype(jnp.bfloat16), 'narrow').astype(jnp.float32)  581 us
    unnamed x16, waiting for transfers between devices  56.9 us
    dot_general x16, matrix products, masked_scores(): jnp.einsum('rhd,chd->hrc', query_pair, key_pair, preferred_element_type=j...  51.8 us
    unnamed x235, local copies, waits for them, and re-layouts  47.6 us
    dot_general x9, matrix products, dot_plain(): jnp.dot(first_factor, second_factor, preferred_element_type=jnp.float32)  43.3 us
    psum x1, blocking collectives, per_device(): lax.psum((grad_vectors, own_squares), ('dp', 'narrow'))  39.8 us
    reduce_scatter x1, waiting for transfers between devices, per_device(): lax.psum_scatter(narrow_up.astype(jnp.bfloat16), 'dp', scatter_dimension=...  36.3 us
    reduce_scatter x1, waiting for transfers between devices, per_device(): lax.psum_scatter(narrow_attn.astype(jnp.bfloat16), 'dp', scatter_dimensio...  36 us
  transfers between devices with their start and end apart: 14, of which 10 were waited for; matrix products, arithmetic and copies ran while one was open for 34% of the time, Pallas kernels for 0%

commit v1 on v0

v1 whole, which is shorter than its diff:
```python
import math

import jax
import jax.numpy as jnp
from jax import lax
from jax.experimental import pallas as pl
from jax.experimental.pallas import tpu as pltpu
from jax.sharding import Mesh, PartitionSpec as P

D = 512
H = 8
FF = 2048
MEM = 512
BANK = 512
KNB = 4
LEN = 1024
CTX = MEM + LEN
ROWS = CTX + BANK
HD = D // H
TB = 256
NT = LEN // TB
MC = MEM // TB
BC = BANK // TB
PAIR = 2 * HD
NPAIR = D // PAIR
F32 = jnp.float32
BF16 = jnp.bfloat16
NS_ITERS = 5
PARAMS = 3150848
epsilon = 1e-06
masked_score = -1e30
coef_first = 3.4445
coef_second = -4.775
coef_third = 2.0315
clip_fraction = 0.05
muon_rate = 0.5
muon_decay = 0.5
vector_rate = 0.5
vector_decay = 0.9
highest = lax.Precision.HIGHEST
VMEM_LIMIT = 60 * 1024 * 1024


def nn(a, b):
    return lax.dot_general(a, b, (((1,), (0,)), ((), ())), preferred_element_type=F32)


def nt(a, b):
    return lax.dot_general(a, b, (((1,), (1,)), ((), ())), preferred_element_type=F32)


def tn(a, b):
    return lax.dot_general(a, b, (((0,), (0,)), ((), ())), preferred_element_type=F32)


def rms_factor(values):
    return lax.rsqrt(jnp.mean(values * values, axis=-1, keepdims=True) + epsilon)


def whole(shape):
    return pl.BlockSpec(shape, lambda *_: (0,) * len(shape))


def call(body, grid, in_specs, out_specs, out_shape, flops, nbytes, name, scratch=(), trans=0, prefetch=0):
    return pl.pallas_call(
        body,
        grid_spec=pltpu.PrefetchScalarGridSpec(
            num_scalar_prefetch=prefetch,
            grid=grid,
            in_specs=in_specs,
            out_specs=out_specs,
            scratch_shapes=list(scratch),
        ),
        out_shape=out_shape,
        name=name,
        cost_estimate=pl.CostEstimate(flops=int(flops), bytes_accessed=int(nbytes), transcendentals=int(trans)),
        compiler_params=pltpu.CompilerParams(
            vmem_limit_bytes=VMEM_LIMIT, dimension_semantics=("arbitrary",) * len(grid)
        ),
    )


SMEM = pl.BlockSpec(memory_space=pltpu.SMEM)


def sds(shape, dtype):
    return jax.ShapeDtypeStruct(shape, dtype)


def context_body(tok_ref, mem_ref, bank_ref, cot_ref, vec_ref, x_ref, xt_ref, cott_ref, gate_ref):
    i = pl.program_id(0)
    gain = vec_ref[0:1, :]

    def put(rows):
        x_ref[...] = rows
        xt_ref[...] = rows.T

    def norm(values):
        wide = values.astype(F32)
        return (wide * rms_factor(wide) * gain).astype(BF16)

    @pl.when(i < MC)
    def _():
        put(norm(mem_ref[...]))

    @pl.when((i >= MC) & (i < MC + NT))
    def _():
        rows = norm(tok_ref[...])
        put(rows)
        logits = nt(vec_ref[2:10, :].astype(BF16), rows)
        gate = jax.nn.sigmoid(logits)
        for p in range(NPAIR):
            gate_ref[p] = gate[2 * p : 2 * p + 2, :]
        cott_ref[...] = cot_ref[...].T

    @pl.when(i >= MC + NT)
    def _():
        put(bank_ref[...])


def context_kernel(tokens, memory, bank, cot, vectors):
    steps = MC + NT + BC
    clip_tok = lambda i: jnp.clip(i - MC, 0, NT - 1)
    return call(
        context_body,
        (steps,),
        [
            pl.BlockSpec((TB, D), lambda i: (clip_tok(i), 0)),
            pl.BlockSpec((TB, D), lambda i: (jnp.minimum(i, MC - 1), 0)),
            pl.BlockSpec((TB, D), lambda i: (jnp.clip(i - MC - NT, 0, BC - 1), 0)),
            pl.BlockSpec((TB, D), lambda i: (clip_tok(i), 0)),
            whole((2 + H, D)),
        ],
        [
            pl.BlockSpec((TB, D), lambda i: (i, 0)),
            pl.BlockSpec((D, TB), lambda i: (0, i)),
            pl.BlockSpec((D, TB), lambda i: (0, clip_tok(i))),
            pl.BlockSpec((NPAIR, 2, TB), lambda i: (0, 0, clip_tok(i))),
        ],
        [sds((ROWS, D), BF16), sds((D, ROWS), BF16), sds((D, LEN), BF16), sds((NPAIR, 2, LEN), F32)],
        1e7,
        8e6,
        "context",
    )(tokens, memory, bank, cot, vectors)


def mask_body(doc_row_ref, doc_col_ref, near_ref, tok_ref, bank_ref):
    i = pl.program_id(0)
    doc_row = doc_row_ref[...]

    @pl.when(i < NT)
    def _():
        keys = lax.broadcasted_iota(jnp.int32, (TB, LEN), 0) + i * TB
        rows = lax.broadcasted_iota(jnp.int32, (TB, LEN), 1)
        seen = (keys <= rows) & (doc_col_ref[...] == doc_row)
        tok_ref[...] = jnp.where(seen, 0.0, masked_score)

    @pl.when(i >= NT)
    def _():
        keys = lax.broadcasted_iota(jnp.int32, (TB, LEN), 0) + (i - NT) * TB
        count = jnp.zeros((TB, LEN), F32)
        for j in range(KNB):
            count = count + jnp.where(near_ref[j : j + 1, :] == keys, 1.0, 0.0)
        bias = jnp.where(count > 0.5, 0.0, masked_score)
        for j in range(2, KNB + 1):
            bias = jnp.where(count > j - 0.5, math.log(j), bias)
        bank_ref[...] = bias


def mask_kernel(doc_row, doc_col, near_t):
    return call(
        mask_body,
        (NT + BC,),
        [
            whole((1, LEN)),
            pl.BlockSpec((TB, 1), lambda i: (jnp.minimum(i, NT - 1), 0)),
            whole((KNB, LEN)),
        ],
        [
            pl.BlockSpec((TB, LEN), lambda i: (jnp.minimum(i, NT - 1), 0)),
            pl.BlockSpec((TB, LEN), lambda i: (jnp.clip(i - NT, 0, BC - 1), 0)),
        ],
        [sds((LEN, LEN), F32), sds((BANK, LEN), F32)],
        1e7,
        7e6,
        "masks",
    )(doc_row, doc_col, near_t)


def each_block(place_ref, chips, planes):
    for core in range(2):
        for chip in range(chips):
            row = ((place_ref[0] ^ chip) * 2 + (place_ref[1] ^ core))
            for plane in range(planes):
                yield core, chip, plane, row, place_ref[2] ^ plane


def part(index, size):
    return pl.ds(pl.multiple_of(index * size, size), size)


def project_rows(i, x_ref, w_ref, q_ref, k_ref, v_ref, kt_ref, vt_ref):
    rows = x_ref[...]
    keys = nn(rows, w_ref[1]).astype(BF16)
    values = nn(rows, w_ref[2]).astype(BF16)
    k_ref[...] = keys
    v_ref[...] = values
    kt_ref[...] = keys.T
    vt_ref[...] = values.T

    @pl.when((i >= MC) & (i < MC + NT))
    def _():
        q_ref[...] = (nn(rows, w_ref[0]).astype(BF16).astype(F32) * (1.0 / math.sqrt(HD))).astype(BF16)


def project_kernel(x, w, place=None):
    steps = MC + NT + BC
    fast = place is not None
    if fast:
        chips, planes = len(w) // 2, w[0].shape[0]
        own_rows, own_cols = w[0].shape[2:]

    def body(*refs):
        i = pl.program_id(0)
        if not fast:
            project_rows(i, *refs)
            return
        place_ref, x_ref, *rest = refs
        blocks, (w_ref, *outs) = rest[: len(w)], rest[len(w) :]

        @pl.when(i == 0)
        def _():
            for core, chip, plane, row, col in each_block(place_ref, chips, planes):
                for j in range(3):
                    w_ref[j, part(row, own_rows), part(col, own_cols)] = blocks[core * chips + chip][plane, j]

        project_rows(i, x_ref, w_ref, *outs)

    out_specs = [
        pl.BlockSpec((TB, D), lambda i: (jnp.clip(i - MC, 0, NT - 1), 0)),
        pl.BlockSpec((TB, D), lambda i: (i, 0)),
        pl.BlockSpec((TB, D), lambda i: (i, 0)),
        pl.BlockSpec((D, TB), lambda i: (0, i)),
        pl.BlockSpec((D, TB), lambda i: (0, i)),
    ]
    out_shape = [
        sds((LEN, D), BF16),
        sds((ROWS, D), BF16),
        sds((ROWS, D), BF16),
        sds((D, ROWS), BF16),
        sds((D, ROWS), BF16),
    ]
    in_specs = [pl.BlockSpec((TB, D), lambda i: (i, 0))]
    if fast:
        in_specs = [SMEM] + in_specs + [whole(b.shape) for b in w]
        out_specs = [whole((3, D, D))] + out_specs
        out_shape = [sds((3, D, D), BF16)] + out_shape
        operands = (place, x, *w)
    else:
        in_specs = in_specs + [whole((3, D, D))]
        operands = (x, w)
    result = call(
        body, (steps,), in_specs, out_specs, out_shape, 2 * D * D * (LEN + 2 * ROWS), 14e6, "project"
    )(*operands)
    return result if fast else [w, *result]


def head_lanes(values, h):
    lanes = lax.broadcasted_iota(jnp.int32, values.shape, 1)
    keep = (lanes < HD) if h == 0 else (lanes >= HD)
    return jnp.where(keep, values, jnp.zeros_like(values))


def key_chunks(tb):
    return list(range(MC + tb + 1)), list(range(MC + NT, MC + NT + BC))


def attend_body(
    q_ref, k_ref, vt_ref, tok_ref, bank_ref, doc_ref, gate_ref,
    e_ref, local_ref, fetched_ref, stat_ref, mixed_ref, mixedt_ref, s_ref,
):
    p = pl.program_id(0)
    for tb in range(NT):
        cols = slice(tb * TB, (tb + 1) * TB)
        q_rows = q_ref[cols, :]
        mem_bias = jnp.where(doc_ref[:, cols] == 0.0, 0.0, masked_score)
        mixed_parts = []
        for h in range(2):
            q_head = head_lanes(q_rows, h)
            head_rows = slice(h * HD, (h + 1) * HD)

            def soft(chunks, slot):
                peak = jnp.full((8, TB), -3e38, F32)
                for c in chunks:
                    keys = slice(c * TB, (c + 1) * TB)
                    s = nt(k_ref[keys, :], q_head)
                    if c < MC:
                        s = s + mem_bias
                    elif c < MC + NT:
                        s = s + tok_ref[(c - MC) * TB : (c - MC + 1) * TB, cols]
                    else:
                        s = s + bank_ref[(c - MC - NT) * TB : (c - MC - NT + 1) * TB, cols]
                    s_ref[slot, keys, :] = s
                    peak = jnp.maximum(peak, jnp.max(s.reshape(TB // 8, 8, TB), axis=0))
                top = jnp.max(peak, axis=0, keepdims=True)
                total = jnp.zeros((8, TB), F32)
                result = jnp.zeros((HD, TB), F32)
                for c in chunks:
                    keys = slice(c * TB, (c + 1) * TB)
                    e = jnp.exp(s_ref[slot, keys, :] - top)
                    total = total + jnp.sum(e.reshape(TB // 8, 8, TB), axis=0)
                    low = e.astype(BF16)
                    e_ref[h, keys, cols] = low
                    result = result + nn(vt_ref[head_rows, keys], low)
                inverse = 1.0 / jnp.sum(total, axis=0, keepdims=True)
                return result * inverse, inverse

            near, far = key_chunks(tb)
            local, local_inv = soft(near, h)
            fetched, fetched_inv = soft(far, h)
            local_ref[head_rows, cols] = local
            fetched_ref[head_rows, cols] = fetched
            stat_ref[0, h : h + 1, cols] = local_inv
            stat_ref[0, 2 + h : 3 + h, cols] = fetched_inv
            gate = gate_ref[0, h : h + 1, cols]
            mixed_parts.append((1.0 - gate) * local + gate * fetched)
        mixed = jnp.concatenate(mixed_parts, axis=0)
        mixedt_ref[:, cols] = mixed.astype(BF16)
        mixed_ref[cols, :] = mixed.T.astype(BF16)


def attend_kernel(q, k, vt, bias_tok, bias_bank, doc_row, gate, first, count):
    spec_cols = lambda rows: pl.BlockSpec((rows, PAIR), lambda p: (0, p + first))
    return call(
        attend_body,
        (count,),
        [
            spec_cols(LEN),
            spec_cols(ROWS),
            pl.BlockSpec((PAIR, ROWS), lambda p: (p + first, 0)),
            whole((LEN, LEN)),
            whole((BANK, LEN)),
            whole((1, LEN)),
            pl.BlockSpec((1, 2, LEN), lambda p: (p + first, 0, 0)),
        ],
        [
            pl.BlockSpec((2, ROWS, LEN), lambda p: (p, 0, 0)),
            pl.BlockSpec((PAIR, LEN), lambda p: (p, 0)),
            pl.BlockSpec((PAIR, LEN), lambda p: (p, 0)),
            pl.BlockSpec((1, 8, LEN), lambda p: (p, 0, 0)),
            pl.BlockSpec((LEN, PAIR), lambda p: (0, p)),
            pl.BlockSpec((PAIR, LEN), lambda p: (p, 0)),
        ],
        [
            sds((2 * count, ROWS, LEN), BF16),
            sds((PAIR * count, LEN), F32),
            sds((PAIR * count, LEN), F32),
            sds((count, 8, LEN), F32),
            sds((LEN, PAIR * count), BF16),
            sds((PAIR * count, LEN), BF16),
        ],
        count * 4 * 2 * PAIR * ROWS * LEN,
        count * 14e6 + 6e6,
        "attend",
        scratch=[pltpu.VMEM((2, ROWS, TB), F32)],
        trans=count * 2 * ROWS * LEN,
    )(q, k, vt, bias_tok, bias_bank, doc_row, gate)


def gelu_parts(x):
    square = jnp.exp(x * x * -0.5)
    z = jnp.abs(x) * 0.7071067811865476
    t = 1.0 / (1.0 + 0.3275911 * z)
    poly = t * (
        0.254829592 + t * (-0.284496736 + t * (1.421413741 + t * (-1.453152027 + t * 1.061405429)))
    )
    tail = 0.5 * poly * square
    cdf = jnp.where(x >= 0.0, 1.0 - tail, tail)
    return cdf, square * 0.3989422804014327


FC = 512


def feed_body(
    mixed_ref, tok_ref, cot_ref, wo_ref, up_ref, dt_ref, vec_ref,
    out_ref, act_ref, gh_ref, ffnt_ref, branch_ref, gres_ref, gmt_ref, gain_ref,
):
    i = pl.program_id(0)
    residual = tok_ref[...].astype(F32) + nn(mixed_ref[...], wo_ref[...])
    factor = rms_factor(residual)
    hat = residual * factor
    gain = vec_ref[1:2, :]
    ffn = (hat * gain).astype(BF16)
    ffnt_ref[...] = ffn.T
    cot = cot_ref[...]
    out = residual
    grad_ffn = jnp.zeros(residual.shape, F32)
    for c in range(FF // FC):
        cols = slice(c * FC, (c + 1) * FC)
        hidden = nn(ffn, up_ref[:, cols])
        cdf, pdf = gelu_parts(hidden)
        act = (hidden * cdf).astype(BF16)
        act_ref[:, cols] = act
        grad_act = nn(cot, dt_ref[:, cols])
        gh = (grad_act * (cdf + hidden * pdf)).astype(BF16)
        gh_ref[:, cols] = gh
        out = out + nt(act, dt_ref[:, cols])
        grad_ffn = grad_ffn + nt(gh, up_ref[:, cols])
    out_ref[...] = out.astype(BF16)
    part = jnp.sum(grad_ffn * hat, axis=0, keepdims=True)

    @pl.when(i == 0)
    def _():
        gain_ref[...] = part

    @pl.when(i > 0)
    def _():
        gain_ref[...] += part

    scaled = grad_ffn * gain
    grad_res = cot.astype(F32) + factor * (scaled - hat * jnp.mean(scaled * hat, axis=-1, keepdims=True))
    gres_ref[...] = grad_res
    branch = grad_res.astype(BF16)
    branch_ref[...] = branch
    gmt_ref[...] = nt(wo_ref[...], branch)


def feed_kernel(mixed, tokens, cot, vectors, w, place=None):
    rows = lambda width: pl.BlockSpec((TB, width), lambda i: (i, 0))
    cols = lambda height: pl.BlockSpec((height, TB), lambda i: (0, i))
    fast = place is not None
    if fast:
        chips, planes = len(w) // 2, w[0].shape[0]
        own_rows, own_o, own_ff = w[0].shape[1], D // planes, FF // planes

    def body(*refs):
        if not fast:
            mixed_ref, tok_ref, cot_ref, vec_ref, wo_ref, up_ref, dt_ref, *outs = refs
            feed_body(mixed_ref, tok_ref, cot_ref, wo_ref, up_ref, dt_ref, vec_ref, *outs)
            return
        place_ref, mixed_ref, tok_ref, cot_ref, vec_ref, *rest = refs
        blocks, outs = rest[: len(w)], rest[len(w) : -3]
        wo_ref, up_ref, dt_ref = rest[-3:]

        @pl.when(pl.program_id(0) == 0)
        def _():
            for core, chip, plane, row, col in each_block(place_ref, chips, planes):
                block = blocks[core * chips + chip]
                here = part(row, own_rows)
                wo_ref[here, part(col, own_o)] = block[plane, :, :own_o]
                up_ref[here, part(col, own_ff)] = block[plane, :, own_o : own_o + own_ff]
                dt_ref[here, part(col, own_ff)] = block[plane, :, own_o + own_ff :]

        feed_body(mixed_ref, tok_ref, cot_ref, wo_ref, up_ref, dt_ref, vec_ref, *outs)

    in_specs = [rows(D), rows(D), rows(D), whole((2 + H, D))] + [whole(b.shape) for b in w]
    scratch = []
    operands = (mixed, tokens, cot, vectors, *w)
    if fast:
        in_specs = [SMEM] + in_specs
        operands = (place, *operands)
        scratch = [pltpu.VMEM((D, D), BF16), pltpu.VMEM((D, FF), BF16), pltpu.VMEM((D, FF), BF16)]
    return call(
        body,
        (NT,),
        in_specs,
        [rows(D), rows(FF), rows(FF), cols(D), rows(D), rows(D), cols(D), whole((1, D))],
        [
            sds((LEN, D), BF16),
            sds((LEN, FF), BF16),
            sds((LEN, FF), BF16),
            sds((D, LEN), BF16),
            sds((LEN, D), BF16),
            sds((LEN, D), F32),
            sds((D, LEN), F32),
            sds((1, D), F32),
        ],
        2 * LEN * D * (4 * FF + 2 * D),
        22e6,
        "feed",
        scratch=scratch,
        trans=LEN * FF * 2,
    )(*operands)


def feed_grads_body(cott_ref, act_ref, ffnt_ref, gh_ref, mixedt_ref, branch_ref, gd_ref, gu_ref, go_ref):
    gd_ref[...] = nn(cott_ref[...], act_ref[...]).astype(BF16)
    gu_ref[...] = nn(ffnt_ref[...], gh_ref[...]).astype(BF16)
    go_ref[...] = nn(mixedt_ref[...], branch_ref[...]).astype(BF16)


def feed_grads_kernel(cot_t, act, ffn_t, gh, mixed_t, branch):
    steps = 4
    wide = lambda width: pl.BlockSpec((LEN, width // steps), lambda i: (0, i))
    out = lambda width: pl.BlockSpec((D, width // steps), lambda i: (0, i))
    return call(
        feed_grads_body,
        (steps,),
        [whole((D, LEN)), wide(FF), whole((D, LEN)), wide(FF), whole((D, LEN)), wide(D)],
        [out(FF), out(FF), out(D)],
        [sds((D, FF), BF16), sds((D, FF), BF16), sds((D, D), BF16)],
        2 * LEN * D * (2 * FF + D),
        17e6,
        "feed_grads",
    )(cot_t, act, ffn_t, gh, mixed_t, branch)


def feed_grads_blocks(cot_t, act, ffn_t, gh, mixed_t, branch, place, chips, planes):
    own_rows, own_o, own_ff = D // (2 * chips), D // planes, FF // planes
    width = own_o + 2 * own_ff

    def body(place_ref, cott_ref, act_ref, ffnt_ref, gh_ref, mixedt_ref, branch_ref, keep_ref, send_ref, all_ref):
        all_ref[:, :own_o] = nn(mixedt_ref[...], branch_ref[...]).astype(BF16)
        all_ref[:, own_o : own_o + own_ff] = nn(ffnt_ref[...], gh_ref[...]).astype(BF16)
        all_ref[:, own_o + own_ff :] = nn(cott_ref[...], act_ref[...]).astype(BF16)
        for chip in range(chips):
            slot = place_ref[0] ^ chip
            keep_ref[slot, 0] = all_ref[part(chip * 2 + place_ref[1], own_rows), :]
            send_ref[slot, 0] = all_ref[part(chip * 2 + 1 - place_ref[1], own_rows), :]

    wide = lambda cols: pl.BlockSpec((LEN, cols // planes), lambda i, _: (0, i))
    out = pl.BlockSpec((chips, 1, own_rows, width), lambda i, place_ref: (0, i ^ place_ref[2], 0, 0))
    shape = sds((chips, planes, own_rows, width), BF16)
    return call(
        body,
        (planes,),
        [whole((D, LEN)), wide(FF), whole((D, LEN)), wide(FF), whole((D, LEN)), wide(D)],
        [out, out],
        [shape, shape],
        2 * LEN * D * (2 * FF + D),
        17e6,
        "feed_grads",
        scratch=[pltpu.VMEM((D, width), BF16)],
        prefetch=1,
    )(place, cot_t, act, ffn_t, gh, mixed_t, branch)


def unattend_body(
    q_ref, k_ref, kt_ref, v_ref, e_ref, gmt_ref, local_ref, fetched_ref, stat_ref, gate_ref,
    dq_ref, dk_ref, dv_ref, gl_ref, ds_ref, do_ref, df_ref, dot_ref,
):
    heads = []
    for h in range(2):
        head_rows = slice(h * HD, (h + 1) * HD)
        gm = gmt_ref[head_rows, :]
        local = local_ref[head_rows, :]
        fetched = fetched_ref[head_rows, :]
        gate = gate_ref[0, h : h + 1, :]
        local_inv = stat_ref[0, h : h + 1, :]
        fetched_inv = stat_ref[0, 2 + h : 3 + h, :]
        grad_gate = jnp.sum(gm * (fetched - local), axis=0, keepdims=True)
        gl_ref[0, h : h + 1, :] = grad_gate * gate * (1.0 - gate)
        grad_local = ((1.0 - gate) * gm).astype(BF16).astype(F32)
        grad_fetched = gate * gm
        do_ref[h] = jnp.zeros((PAIR, LEN), BF16)
        df_ref[h] = jnp.zeros((PAIR, LEN), BF16)
        do_ref[h, head_rows, :] = (grad_local * local_inv).astype(BF16)
        df_ref[h, head_rows, :] = (grad_fetched * fetched_inv).astype(BF16)
        dot_ref[h : h + 1, :] = jnp.sum(grad_local * local, axis=0, keepdims=True) * local_inv
        dot_ref[2 + h : 3 + h, :] = jnp.sum(grad_fetched * fetched, axis=0, keepdims=True) * fetched_inv
    for tb in range(NT):
        cols = slice(tb * TB, (tb + 1) * TB)
        near, far = key_chunks(tb)
        dq_parts = []
        for h in range(2):
            head_rows = slice(h * HD, (h + 1) * HD)
            dq = jnp.zeros((HD, TB), F32)
            for c in near + far:
                keys = slice(c * TB, (c + 1) * TB)
                bank = c >= MC + NT
                grad_out = (df_ref if bank else do_ref)[h, :, cols]
                row = 2 + h if bank else h
                gp = nn(v_ref[keys, :], grad_out) - dot_ref[row : row + 1, cols]
                ds = (e_ref[h, keys, cols].astype(F32) * gp).astype(BF16)
                ds_ref[h, keys, cols] = ds
                dq = dq + nn(kt_ref[head_rows, keys], ds)
            dq_parts.append(dq)
        dq_pair = jnp.concatenate(dq_parts, axis=0) * (1.0 / math.sqrt(HD))
        dq_ref[cols, :] = dq_pair.T.astype(BF16)
    for c in range(ROWS // TB):
        keys = slice(c * TB, (c + 1) * TB)
        bank = c >= MC + NT
        start = (c - MC) * TB if MC <= c < MC + NT else 0
        dk = jnp.zeros((TB, PAIR), F32)
        dv = jnp.zeros((TB, PAIR), F32)
        for h in range(2):
            grad_out = (df_ref if bank else do_ref)[h, :, start:]
            dv = dv + nt(e_ref[h, keys, start:], grad_out)
            dk = dk + nn(ds_ref[h, keys, start:], head_lanes(q_ref[start:, :], h))
        dk_ref[keys, :] = dk.astype(BF16)
        dv_ref[keys, :] = dv.astype(BF16)


def unattend_kernel(q, k, kt, v, e, gmt, local, fetched, stat, gate, first, count):
    spec_cols = lambda rows: pl.BlockSpec((rows, PAIR), lambda p: (0, p + first))
    spec_rows = lambda cols: pl.BlockSpec((PAIR, cols), lambda p: (p + first, 0))
    own_rows = lambda cols: pl.BlockSpec((PAIR, cols), lambda p: (p, 0))
    own_cols = lambda rows: pl.BlockSpec((rows, PAIR), lambda p: (0, p))
    return call(
        unattend_body,
        (count,),
        [
            spec_cols(LEN),
            spec_cols(ROWS),
            spec_rows(ROWS),
            spec_cols(ROWS),
            pl.BlockSpec((2, ROWS, LEN), lambda p: (p, 0, 0)),
            spec_rows(LEN),
            own_rows(LEN),
            own_rows(LEN),
            pl.BlockSpec((1, 8, LEN), lambda p: (p, 0, 0)),
            pl.BlockSpec((1, 2, LEN), lambda p: (p + first, 0, 0)),
        ],
        [
            own_cols(LEN),
            own_cols(ROWS),
            own_cols(ROWS),
            pl.BlockSpec((1, 2, LEN), lambda p: (p, 0, 0)),
        ],
        [
            sds((LEN, PAIR * count), BF16),
            sds((ROWS, PAIR * count), BF16),
            sds((ROWS, PAIR * count), BF16),
            sds((count, 2, LEN), F32),
        ],
        count * 4 * 4 * PAIR * ROWS * LEN,
        count * 14e6,
        "unattend",
        scratch=[
            pltpu.VMEM((2, ROWS, LEN), BF16),
            pltpu.VMEM((2, PAIR, LEN), BF16),
            pltpu.VMEM((2, PAIR, LEN), BF16),
            pltpu.VMEM((8, LEN), F32),
        ],
    )(q, k, kt, v, e, gmt, local, fetched, stat, gate)


def all_heads(gl_ref):
    return jnp.concatenate([gl_ref[p] for p in range(NPAIR)], axis=0).astype(BF16)


def proj_grads_body(xt_ref, dq_ref, dk_ref, dv_ref, gl_ref, g_ref, gate_ref):
    g_ref[0] = nn(xt_ref[:, MEM:CTX], dq_ref[...]).astype(BF16)
    g_ref[1] = nn(xt_ref[...], dk_ref[...]).astype(BF16)
    g_ref[2] = nn(xt_ref[...], dv_ref[...]).astype(BF16)

    @pl.when(pl.program_id(0) == 0)
    def _():
        gate_ref[...] = nt(all_heads(gl_ref), xt_ref[:, MEM:CTX])


def proj_grads_kernel(xt, dq, dk, dv, gl, place=None, chips=0, planes=0):
    steps = 2
    fast = place is not None
    wide = lambda rows: pl.BlockSpec((rows, D // steps), lambda i, *_: (0, i))
    in_specs = [whole((D, ROWS)), wide(LEN), wide(ROWS), wide(ROWS), whole((NPAIR, 2, LEN))]
    gate_spec, gate_shape = whole((H, D)), sds((H, D), F32)
    flops, nbytes = 2 * D * D * (LEN + 2 * ROWS), 10e6
    if not fast:
        return call(
            proj_grads_body,
            (steps,),
            in_specs,
            [pl.BlockSpec((3, D, D // steps), lambda i: (0, 0, i)), gate_spec],
            [sds((3, D, D), BF16), gate_shape],
            flops,
            nbytes,
            "proj_grads",
        )(xt, dq, dk, dv, gl)
    own_rows, own_cols, group = D // (2 * chips), D // planes, planes // steps

    def body(place_ref, xt_ref, dq_ref, dk_ref, dv_ref, gl_ref, keep_ref, send_ref, gate_ref, all_ref):
        proj_grads_body(xt_ref, dq_ref, dk_ref, dv_ref, gl_ref, all_ref, gate_ref)
        for b in range(group):
            col = b ^ (place_ref[2] % group)
            cols = slice(b * own_cols, (b + 1) * own_cols)
            for chip in range(chips):
                slot = place_ref[0] ^ chip
                for j in range(3):
                    keep_ref[slot, col, j] = all_ref[j, part(chip * 2 + place_ref[1], own_rows), cols]
                    send_ref[slot, col, j] = all_ref[j, part(chip * 2 + 1 - place_ref[1], own_rows), cols]

    out = pl.BlockSpec(
        (chips, group, 3, own_rows, own_cols), lambda i, place_ref: (0, i ^ (place_ref[2] // group), 0, 0, 0)
    )
    shape = sds((chips, planes, 3, own_rows, own_cols), BF16)
    return call(
        body,
        (steps,),
        in_specs,
        [out, out, gate_spec],
        [shape, shape, gate_shape],
        flops,
        nbytes,
        "proj_grads",
        scratch=[pltpu.VMEM((3, D, D // steps), BF16)],
        prefetch=1,
    )(place, xt, dq, dk, dv, gl)


def input_body(dq_ref, dk_ref, dv_ref, gl_ref, w_ref, tok_ref, mem_ref, vec_ref, gres_ref, gin_ref, gain_ref):
    i = pl.program_id(0)
    gn = nt(dk_ref[...], w_ref[1]) + nt(dv_ref[...], w_ref[2])

    @pl.when(i < MC)
    def _():
        wide = mem_ref[...].astype(F32)
        part = jnp.sum(gn * (wide * rms_factor(wide)), axis=0, keepdims=True)

        @pl.when(i == 0)
        def _():
            gain_ref[...] = part

        @pl.when(i > 0)
        def _():
            gain_ref[...] += part

    @pl.when(i >= MC)
    def _():
        wide = tok_ref[...].astype(F32)
        factor = rms_factor(wide)
        hat = wide * factor
        full = gn + nt(dq_ref[...], w_ref[0]) + tn(all_heads(gl_ref), vec_ref[2:10, :].astype(BF16))
        gain_ref[...] += jnp.sum(full * hat, axis=0, keepdims=True)
        scaled = full * vec_ref[0:1, :]
        gin_ref[...] = (
            gres_ref[...] + factor * (scaled - hat * jnp.mean(scaled * hat, axis=-1, keepdims=True))
        ).astype(BF16)


def input_kernel(dq, dk, dv, gl, w, tokens, memory, vectors, gres):
    tok = lambda i: jnp.clip(i - MC, 0, NT - 1)
    rows = pl.BlockSpec((TB, D), lambda i: (tok(i), 0))
    return call(
        input_body,
        (MC + NT,),
        [
            rows,
            pl.BlockSpec((TB, D), lambda i: (i, 0)),
            pl.BlockSpec((TB, D), lambda i: (i, 0)),
            pl.BlockSpec((NPAIR, 2, TB), lambda i: (0, 0, tok(i))),
            whole((3, D, D)),
            rows,
            pl.BlockSpec((TB, D), lambda i: (jnp.minimum(i, MC - 1), 0)),
            whole((2 + H, D)),
            rows,
        ],
        [rows, whole((1, D))],
        [sds((LEN, D), BF16), sds((1, D), F32)],
        2 * D * D * (LEN + 2 * CTX),
        10e6,
        "input",
    )(dq, dk, dv, gl, w, tokens, memory, vectors, gres)


def exchange(slots, axis):
    size = len(slots)
    return [slots[0]] + [
        lax.ppermute(slots[r], axis, [(i, i ^ r) for i in range(size)]) for r in range(1, size)
    ]


def gather_blocks(block, chips, planes):
    column = jnp.stack(exchange([block] * planes, "narrow"))
    plane = exchange([column] * chips, "chip")
    return plane + [exchange([b, b], "core")[1] for b in plane]


def added(parts):
    total = parts[0].astype(F32)
    for other in parts[1:]:
        total = total + other.astype(F32)
    return total


def scatter_core(keep, send):
    other = exchange([send, send], "core")[1]
    return [added([keep[r], other[r]]).astype(BF16) for r in range(keep.shape[0])]


def scatter_chips(slots):
    total = added(exchange(slots, "chip")).astype(BF16)
    return [total[r] for r in range(total.shape[0])]


PLANES = (("up",), ("q", "k"), ("v", "o"), ("down",))


def owned_kernel(parts_a, parts_b, devices):
    count = len(parts_a)

    def body(*refs):
        a_refs, b_refs, (ga_ref, gb_ref, sq_ref) = refs[:count], refs[count : 2 * count], refs[2 * count :]
        ga = added([r[...] for r in a_refs])
        gb = added([r[...] for r in b_refs])
        ga_ref[...] = ga
        gb_ref[...] = gb
        squares = jnp.sum(ga * ga) + jnp.sum(gb * gb)
        sq_ref[...] = jnp.full(sq_ref.shape, 1.0, F32) * squares

    shape_a, shape_b, shape_sq = parts_a[0].shape, parts_b[0].shape, (devices, 8, 128)
    return call(
        body,
        (1,),
        [whole(shape_a)] * count + [whole(shape_b)] * count,
        [whole(shape_a), whole(shape_b), whole(shape_sq)],
        [sds(shape_a, F32), sds(shape_b, F32), sds(shape_sq, F32)],
        1e6,
        2e6,
        "owned",
    )(*parts_a, *parts_b)


def moment_kernel(place, sq_all, vec_a, vec_b, vectors, vec_moment, ga, gb, attn_moment, up_moment, down_moment):
    own_rows, own_cols = attn_moment.shape[1:]
    own_ff = up_moment.shape[1]
    planes = len(PLANES)
    limit = clip_fraction * math.sqrt(PARAMS)

    def body(
        place_ref, sq_ref, va_ref, vb_ref, vec_ref, vm_ref, ga_ref, gb_ref, am_ref, um_ref, dm_ref,
        an_ref, un_ref, dn_ref, vn_ref, vmn_ref, norm_ref, *rest,
    ):
        slot_refs, all_ref = rest[:planes], rest[planes]
        grad_vec = va_ref[...] + vb_ref[...]
        total = jnp.sum(sq_ref[...], axis=0)[0:1, 0:1] + jnp.sum(grad_vec * grad_vec)
        norm = jnp.sqrt(total)
        norm_ref[...] = norm
        clip = limit / jnp.maximum(norm, limit)
        vec_mom = vector_decay * vm_ref[...] + clip * grad_vec
        vmn_ref[...] = vec_mom
        vn_ref[...] = vec_ref[...] - vector_rate * vec_mom
        all_ref[...] = jnp.zeros(all_ref.shape, BF16)
        for j in range(4):
            grad = ga_ref[j] if j < 3 else gb_ref[:, :own_cols]
            mom = muon_decay * am_ref[j] + clip * grad
            an_ref[j] = mom
            all_ref[1 + j // 2, :, (j % 2) * own_cols : (j % 2 + 1) * own_cols] = mom.astype(BF16)
        mom = muon_decay * um_ref[...] + clip * gb_ref[:, own_cols : own_cols + own_ff]
        un_ref[...] = mom
        all_ref[0] = mom.astype(BF16)
        mom = muon_decay * dm_ref[...].T + clip * gb_ref[:, own_cols + own_ff :]
        dn_ref[...] = mom.T
        all_ref[3] = mom.astype(BF16)
        for r in range(planes):
            slot_refs[r][...] = all_ref[place_ref[2] ^ r]

    slot = sds((own_rows, own_ff), BF16)
    operands = (sq_all, vec_a, vec_b, vectors, vec_moment, ga, gb, attn_moment, up_moment, down_moment)
    shapes = [
        sds(attn_moment.shape, F32),
        sds(up_moment.shape, F32),
        sds(down_moment.shape, F32),
        sds(vectors.shape, F32),
        sds(vectors.shape, F32),
        sds((1, 1), F32),
    ] + [slot] * planes
    return call(
        body,
        (1,),
        [SMEM] + [whole(x.shape) for x in operands],
        [whole(x.shape) for x in shapes],
        shapes,
        1e6,
        2e6,
        "moment",
        scratch=[pltpu.VMEM((planes, own_rows, own_ff), BF16)],
    )(place, *operands)


def orthogonal_kernel(place, blocks):
    chips = len(blocks) // 2
    planes, own_rows, own_ff = blocks[0].shape
    own_cols = D // planes

    def body(place_ref, *refs):
        block_refs, out_refs = refs[: len(blocks)], refs[len(blocks) : len(blocks) + planes]
        low_ref, x_ref, mix_ref, all_ref = refs[len(blocks) + planes :]
        pair = (place_ref[2] == 1) | (place_ref[2] == 2)
        own = part(place_ref[0] * 2 + place_ref[1], own_rows)

        def iterate(step, start, width, scale):
            cols = slice(start, start + width)
            gram = nt(low_ref[:, cols], low_ref[:, cols])
            if step == 0:
                eye = lax.broadcasted_iota(jnp.int32, (D, D), 0) == lax.broadcasted_iota(jnp.int32, (D, D), 1)
                scale = 1.0 / (jnp.sqrt(jnp.sum(jnp.where(eye, gram, 0.0))) + 1e-07)
                gram = gram * (scale * scale)
            low = gram.astype(BF16)
            mix = (coef_second * gram + coef_third * nn(low, low)).astype(BF16)
            mix_ref[:, :] = mix
            for c in range(start, start + width, D):
                some = slice(c, c + D)
                if step < NS_ITERS - 1:
                    old = low_ref[:, some].astype(F32) if step == 0 else x_ref[:, some]
                    new = coef_first * old + nn(mix_ref[...], low_ref[:, some])
                    if step == 0:
                        new = new * scale
                    x_ref[:, some] = new
                    low_ref[:, some] = new.astype(BF16)
                else:
                    x_ref[own, some] = coef_first * x_ref[own, some] + nn(mix_ref[own, :], low_ref[:, some])
            return scale

        @pl.when(pair)
        def _():
            for core, chip, plane, row, col in each_block(place_ref, chips, planes):
                for j in range(2):
                    low_ref[part(row, own_rows), part(col + j * planes, own_cols)] = block_refs[core * chips + chip][
                        plane, :, j * own_cols : (j + 1) * own_cols
                    ]
            scales = [None, None]
            for step in range(NS_ITERS):
                for j in range(2):
                    scales[j] = iterate(step, j * D, D, scales[j])
            for plane in range(planes):
                for j in range(2):
                    first = j * D + plane * own_cols
                    all_ref[plane, :, j * own_cols : (j + 1) * own_cols] = x_ref[own, first : first + own_cols].astype(
                        BF16
                    )

        @pl.when(jnp.logical_not(pair))
        def _():
            for core, chip, plane, row, col in each_block(place_ref, chips, planes):
                low_ref[part(row, own_rows), part(col, own_ff)] = block_refs[core * chips + chip][plane]
            scale = None
            for step in range(NS_ITERS):
                scale = iterate(step, 0, FF, scale)
            for plane in range(planes):
                all_ref[plane] = x_ref[own, plane * own_ff : (plane + 1) * own_ff].astype(BF16)

        for r in range(planes):
            out_refs[r][...] = all_ref[place_ref[2] ^ r]

    slot = sds((own_rows, own_ff), BF16)
    return call(
        body,
        (1,),
        [SMEM] + [whole(b.shape) for b in blocks],
        [whole(slot.shape)] * planes,
        [slot] * planes,
        12e9,
        3e6,
        "orthogonal",
        scratch=[
            pltpu.VMEM((D, FF), BF16),
            pltpu.VMEM((D, FF), F32),
            pltpu.VMEM((D, D), BF16),
            pltpu.VMEM((planes, own_rows, own_ff), BF16),
        ],
    )(place, *blocks)


def update_kernel(place, slots, attn_weights, up_weights, down_weights):
    planes = len(slots)
    own_rows, own_cols = attn_weights.shape[1:]
    shape_factor = math.sqrt(max(1.0, FF / D))

    def body(place_ref, *refs):
        slot_refs, (aw_ref, uw_ref, dw_ref, an_ref, un_ref, dn_ref, all_ref) = refs[:planes], refs[planes:]
        for r in range(planes):
            all_ref[place_ref[2] ^ r] = slot_refs[r][...]
        for j in range(4):
            ortho = all_ref[1 + j // 2, :, (j % 2) * own_cols : (j % 2 + 1) * own_cols].astype(F32)
            an_ref[j] = aw_ref[j] - muon_rate * ortho
        un_ref[...] = uw_ref[...] - muon_rate * all_ref[0].astype(F32)
        dn_ref[...] = dw_ref[...] - muon_rate * shape_factor * all_ref[3].astype(F32).T

    weights = (attn_weights, up_weights, down_weights)
    return call(
        body,
        (1,),
        [SMEM] + [whole(x.shape) for x in slots] + [whole(x.shape) for x in weights],
        [whole(x.shape) for x in weights],
        [sds(x.shape, F32) for x in weights],
        1e6,
        2e6,
        "update",
        scratch=[pltpu.VMEM((planes,) + slots[0].shape, BF16)],
    )(place, *slots, *weights)


def local_start(tokens, memory, bank, starts, near, cot, vectors):
    doc = jnp.cumsum(starts).astype(F32)
    x, xt, cot_t, gate = context_kernel(tokens, memory, bank, cot, vectors)
    doc_row = doc.reshape(1, LEN)
    bias_tok, bias_bank = mask_kernel(doc_row, doc.reshape(LEN, 1), near.T)
    return x, xt, cot_t, gate, doc_row, bias_tok, bias_bank


def plain_tail(sizes, grads, attn_weights, up_weights, down_weights, vectors, attn_moment, up_moment, down_moment, vec_moment):
    dp = ("chip", "core")
    grad_attn, grad_up, grad_down, grad_vectors = grads

    def owned(grad, narrow_dim, dp_dim):
        part_sum = lax.psum_scatter(grad.astype(BF16), "narrow", scatter_dimension=narrow_dim, tiled=True)
        return lax.psum_scatter(part_sum, dp, scatter_dimension=dp_dim, tiled=True).astype(F32)

    owned_attn, owned_up, owned_down = owned(grad_attn, 2, 1), owned(grad_up, 1, 0), owned(grad_down, 0, 1)
    own_squares = jnp.sum(owned_attn * owned_attn) + jnp.sum(owned_up * owned_up) + jnp.sum(owned_down * owned_down)
    vector_sum, square_sum = lax.psum((grad_vectors, own_squares), ("chip", "core", "narrow"))
    grad_norm = jnp.sqrt(square_sum + jnp.sum(vector_sum * vector_sum))
    clip_limit = clip_fraction * math.sqrt(PARAMS)
    clip_factor = clip_limit / jnp.maximum(grad_norm, clip_limit)
    attn_mom_new = muon_decay * attn_moment + clip_factor * owned_attn
    up_mom_new = muon_decay * up_moment + clip_factor * owned_up
    down_mom_new = muon_decay * down_moment + clip_factor * owned_down
    gather = lambda x, dim: lax.all_gather(x.astype(BF16), dp, axis=dim, tiled=True).astype(F32)
    ortho = (gather(attn_mom_new, 1), gather(up_mom_new, 0), gather(down_mom_new, 1))
    ortho_attn, ortho_up, ortho_down = ortho
    for iteration in range(NS_ITERS):
        gram_attn = jnp.einsum("imc,inc->imn", ortho_attn, ortho_attn, precision=highest)
        gram_up = lax.dot_general(ortho_up, ortho_up, (((1,), (1,)), ((), ())), precision=highest)
        gram_down = lax.dot_general(ortho_down, ortho_down, (((0,), (0,)), ((), ())), precision=highest)
        partial_grams = jnp.concatenate([gram_attn, gram_up[None], gram_down[None]], axis=0)
        gram_total = lax.psum(partial_grams.astype(BF16), "narrow").astype(F32)
        if iteration == 0:
            norm_scales = 1.0 / (jnp.sqrt(jnp.trace(gram_total, axis1=1, axis2=2)) + 1e-07)
            ortho_attn = ortho_attn * norm_scales[:4, None, None]
            ortho_up = ortho_up * norm_scales[4]
            ortho_down = ortho_down * norm_scales[5]
            gram_total = gram_total * (norm_scales * norm_scales)[:, None, None]
        once = jnp.einsum("imn,inc->imc", gram_total[:4], ortho_attn, precision=highest)
        twice = jnp.einsum("imn,inc->imc", gram_total[:4], once, precision=highest)
        ortho_attn = coef_first * ortho_attn + coef_second * once + coef_third * twice
        once = jnp.dot(gram_total[4], ortho_up, precision=highest)
        twice = jnp.dot(gram_total[4], once, precision=highest)
        ortho_up = coef_first * ortho_up + coef_second * once + coef_third * twice
        once = jnp.dot(ortho_down, gram_total[5], precision=highest)
        twice = jnp.dot(once, gram_total[5], precision=highest)
        ortho_down = coef_first * ortho_down + coef_second * once + coef_third * twice
    row_share = D // sizes["dp"]
    row_start = lax.axis_index(dp) * row_share
    final_attn = lax.dynamic_slice_in_dim(ortho_attn, row_start, row_share, 1)
    final_up = lax.dynamic_slice_in_dim(ortho_up, row_start, row_share, 0)
    final_down = lax.dynamic_slice_in_dim(ortho_down, row_start, row_share, 1)
    shape_factor = math.sqrt(max(1.0, FF / D))
    vector_mom_new = vector_decay * vec_moment + clip_factor * vector_sum
    return (
        attn_weights - muon_rate * final_attn,
        up_weights - muon_rate * final_up,
        down_weights - muon_rate * shape_factor * final_down,
        attn_mom_new,
        up_mom_new,
        down_mom_new,
        vectors - vector_rate * vector_mom_new,
        vector_mom_new,
        grad_norm,
    )


def per_device(
    sizes,
    tokens, memory, neighbour_bank, starts, neighbours, cotangent,
    attn_weights, up_weights, down_weights, vectors,
    attn_moment, up_moment, down_moment, vector_moment,
):
    chips, planes = sizes["dp"] // 2, sizes["narrow"]
    fast = planes == len(PLANES) and chips == 4
    memory = memory.reshape(MEM, D)
    bank = neighbour_bank.reshape(BANK, D)
    attn_low = attn_weights.astype(BF16)
    if fast:
        place = jnp.stack([lax.axis_index("chip"), lax.axis_index("core"), lax.axis_index("narrow")]).astype(jnp.int32)
        first = gather_blocks(attn_low[:3], chips, planes)
        rest = jnp.concatenate([attn_low[3], up_weights.astype(BF16), down_weights.T.astype(BF16)], axis=1)
        second = gather_blocks(rest, chips, planes)
    else:
        place = None
        full = lambda x, narrow_dim, dp_dim: lax.all_gather(
            lax.all_gather(x, ("chip", "core"), axis=dp_dim, tiled=True), "narrow", axis=narrow_dim, tiled=True
        )
        attn_full = full(attn_low, 2, 1)
        first = attn_full[:3]
        second = [attn_full[3], full(up_weights.astype(BF16), 1, 0), full(down_weights.astype(BF16), 0, 1).T]
    x, xt, cot_t, gate, doc_row, bias_tok, bias_bank = local_start(
        tokens, memory, bank, starts, neighbours, cotangent, vectors
    )
    w, q, k, v, kt, vt = project_kernel(x, first, place)
    e, local, fetched, stat, mixed, mixed_t = attend_kernel(q, k, vt, bias_tok, bias_bank, doc_row, gate, 0, NPAIR)
    out, act, gh, ffn_t, branch, gres, gmt, gain_ffn = feed_kernel(mixed, tokens, cotangent, vectors, second, place)
    if fast:
        keep_b, send_b = feed_grads_blocks(cot_t, act, ffn_t, gh, mixed_t, branch, place, chips, planes)
        slots_b = scatter_chips(scatter_core(keep_b, send_b))
    else:
        grad_down_t, grad_up, grad_o = feed_grads_kernel(cot_t, act, ffn_t, gh, mixed_t, branch)
    dq, dk, dv, gl = unattend_kernel(q, k, kt, v, e, gmt, local, fetched, stat, gate, 0, NPAIR)
    if fast:
        keep_a, send_a, grad_gate = proj_grads_kernel(xt, dq, dk, dv, gl, place, chips, planes)
    else:
        grad_qkv, grad_gate = proj_grads_kernel(xt, dq, dk, dv, gl)
    grad_in, gain_attn = input_kernel(dq, dk, dv, gl, w, tokens, memory, vectors, gres)
    grad_vectors = jnp.concatenate([gain_attn, gain_ffn, grad_gate], axis=0)
    if not fast:
        grads = (jnp.concatenate([grad_qkv, grad_o[None]], axis=0), grad_up, grad_down_t.T, grad_vectors)
        return (out, grad_in) + plain_tail(
            sizes, grads, attn_weights, up_weights, down_weights, vectors,
            attn_moment, up_moment, down_moment, vector_moment,
        )
    slots_a = scatter_core(keep_a, send_a)
    vec_chip = added(exchange([grad_vectors] * chips, "chip"))
    slots_a = scatter_chips(slots_a)
    vec_plane = added(exchange([vec_chip] * planes, "narrow"))
    vec_other = exchange([vec_plane, vec_plane], "core")[1]
    parts_a, parts_b = exchange(slots_a, "narrow"), exchange(slots_b, "narrow")
    ga, gb, squares = owned_kernel(parts_a, parts_b, chips * 2 * planes)
    sq_all = lax.all_to_all(squares, ("chip", "core", "narrow"), 0, 0)
    attn_mom, up_mom, down_mom, vec_new, vec_mom, norm, *slots = moment_kernel(
        place, sq_all, vec_plane, vec_other, vectors, vector_moment, ga, gb, attn_moment, up_moment, down_moment
    )
    columns = jnp.stack(exchange(slots, "narrow"))
    plane_blocks = exchange([columns] * chips, "chip")
    plane_blocks = plane_blocks + [exchange([b, b], "core")[1] for b in plane_blocks]
    final = exchange(orthogonal_kernel(place, plane_blocks), "narrow")
    attn_new, up_new, down_new = update_kernel(place, final, attn_weights, up_weights, down_weights)
    return (
        out, grad_in, attn_new, up_new, down_new, attn_mom, up_mom, down_mom, vec_new, vec_mom, norm.reshape(()),
    )


def solution(mesh):
    sizes = dict(mesh.shape)
    split = Mesh(
        mesh.devices.reshape(sizes["dp"] // 2, 2, sizes["narrow"]), ("chip", "core", "narrow")
    )
    dp = ("chip", "core")
    rows = ("chip", "core", "narrow")
    weights = (P(None, dp, "narrow"), P(dp, "narrow"), P("narrow", dp))
    return jax.shard_map(
        lambda *operands: per_device(sizes, *operands),
        mesh=split,
        in_specs=(P(rows, None), P(rows, None, None), P(rows, None, None), P(rows), P(rows, None), P(rows, None))
        + weights + (P(),) + weights + (P(),),
        out_specs=(P(rows, None), P(rows, None)) + weights + weights + (P(), P(), P()),
        check_vma=False,
    )
```

time: 1550 us -> 341 us (0.22)
  waiting for transfers between devices: 721 us -> 59.5 us
  matrix products: 344 us -> 0 us
  local copies, waits for them, and re-layouts: 209 us -> 11 us
  Pallas kernels: 0 us -> 189 us
  other arithmetic: 143 us -> 9.24 us
  blocking collectives: 103 us -> 0 us
  starting transfers between devices: 0.58 us -> 67.3 us
  between operations: 20.2 us -> 1.43 us
    psum x5 -> x0, waiting for transfers between devices: 581 us -> none  [per_device(): lax.psum(partial_grams.astype(jnp.bfloat16), 'narrow').astype(jnp.float32)]
    dot_general x126 -> x0, matrix products: 344 us -> none  [the longest x16 51.8 us: masked_scores(): jnp.einsum('rhd,chd->hrc', query_pair, key_pair, preferred_element_type=j...]
    pallas_call x0 -> x13, Pallas kernels: none -> 189 us  [the longest x1 41.3 us: unattend_kernel(): call(unattend_body, (count,), [spec_cols(LEN), spec_cols(ROWS), spec_rows...]
    reduce_scatter x4 -> x0, waiting for transfers between devices: 72.3 us -> none  [the longest x1 36.3 us: per_device(): lax.psum_scatter(narrow_up.astype(jnp.bfloat16), 'dp', scatter_dimension=...]
    gather x6 -> x0, local copies, waits for them, and re-layouts: 64 us -> none  [the longest x3 32.1 us: segment_forward(): jnp.take(bank_values, seg_near, axis=0).reshape(LEN, KNB, H, head_dim)]
    all_gather x6 -> x0, blocking collectives: 62.8 us -> none  [the longest x1 12.4 us: per_device(): lax.all_gather(attn_low, 'dp', axis=1, tiled=True)]
    ppermute x0 -> x54, starting transfers between devices: none -> 61.9 us  [exchange(): lax.ppermute(slots[r], axis, [(i, i ^ r) for i in range(size)])]
    mul x4 -> x0, local copies, waits for them, and re-layouts: 61.4 us -> none  [the longest x2 31 us: segment_backward(): grad_near_values = near_probs[..., None] * grad_fetched[:, None]]
  transfers between devices with their start and end apart: 14 -> 55, of which waited for: 10 -> 18; matrix products, arithmetic and copies ran while one was open for 34% -> 4% of each run, Pallas kernels for 0% -> 36%
where the time goes in v1:
time: 341 us; the launch traced here: 338 us
  Pallas kernels  189 us (55%)
  starting transfers between devices  67.3 us (20%)
  waiting for transfers between devices  59.5 us (17%)
  local copies, waits for them, and re-layouts  11 us (3%)
  other arithmetic  9.24 us (3%)
    ppermute x54, starting transfers between devices, exchange(): lax.ppermute(slots[r], axis, [(i, i ^ r) for i in range(size)])  61.9 us
    ppermute x54, waiting for transfers between devices, exchange(): lax.ppermute(slots[r], axis, [(i, i ^ r) for i in range(size)])  52.4 us
    pallas_call x1, Pallas kernels, unattend_kernel(): call(unattend_body, (count,), [spec_cols(LEN), spec_cols(ROWS), spec_rows...  41.3 us
    pallas_call x1, Pallas kernels, attend_kernel(): call(attend_body, (count,), [spec_cols(LEN), spec_cols(ROWS), pl.BlockSpe...  37.1 us
    pallas_call x1, Pallas kernels, feed_kernel(): call(body, (NT,), in_specs, [rows(D), rows(FF), rows(FF), cols(D), rows(D...  34.5 us
    pallas_call x1, Pallas kernels, orthogonal_kernel(): call(body, (1,), [SMEM] + [whole(b.shape) for b in blocks], [whole(slot.s...  15.4 us
    pallas_call x1, Pallas kernels, feed_grads_blocks(): call(body, (planes,), [whole((D, LEN)), wide(FF), whole((D, LEN)), wide(F...  12 us
    pallas_call x1, Pallas kernels, project_kernel(): call(body, (steps,), in_specs, out_specs, out_shape, 2 * D * D * (LEN + 2...  10.8 us
  transfers between devices with their start and end apart: 55, of which 18 were waited for; matrix products, arithmetic and copies ran while one was open for 4% of the time, Pallas kernels for 36%

profile of v1, /device:TPU:0, one launch (start us, length us, event | category | flops | bytes accessed | tf_op | source)
XLA Modules:
  0.0 337.9 jit_solution(9469735764489490276)
XLA Ops:
  1.6 3.1 collective-permute-start
  4.7 2.6 collective-permute-start.1
  10.6 2.6 collective-permute-done.2
  13.2 1.6 collective-permute-start.3
  16.1 3.1 collective-permute-start.12
  20.4 1.6 collective-permute-start.4
  23.2 4.2 %collective-permute-done.11 = bf16[64,1152]{1,0:T(8,128)(2,1)S(1)} collective-permute-done((bf16[64,1152]{1,0:T(8,128)(2,1)S(1)}, bf16[64,1152]{1,0:T(8,128)(2,1)S(1)}, u32[]{:S(2)}, u32[]{:S(2)}) %collective-permute-start.11) | collective-permute-done | bytes 147488 | tf_op jit(solution)/shard_map/ppermute | solution.py:760
  28.7 1.5 collective-permute-start.14
  33.5 6.1 %masks.1 = (f32[1024,1024]{1,0:T(8,128)}, f32[512,1024]{1,0:T(8,128)}) custom-call(f32[1,1024]{1,0:T(1,128)} %bitcast.80, f32[1024,1]{1,0:T(8,128)} %copy.29.doc_col_ref, s32[4,1024]{1,0:T(4,128)} %bitcast.82), custom_call_target="tpu_custom_call" | custom-call | flops 10000000 | bytes 7000000 | tf_op jit(solution)/shard_map/masks/pallas_call | solution.py:171
  39.6 7.6 %context.1 = (bf16[2048,512]{1,0:T(8,128)(2,1)}, bf16[512,2048]{1,0:T(8,128)(2,1)}, bf16[512,1024]{1,0:T(8,128)(2,1)}, f32[4,2,1024]{2,1,0:T(2,128)}) custom-call(bf16[1024,512]{1,0:T(8,128)(2,1)} %tok_ref.3, bf16[512,512]{1,0:T(8,128)(2,1)} %bitcast.66, bf16[512,512]{1,0:T(8,128)(2,1)} %bitcast.68, bf16[1024,512]{1,0:T(8,128)(2,1)} %refs_3_.1, ...), custom_call_target="tpu_custom_call" | custom-call | flops 10000000 | bytes 8000000 | tf_op jit(solution)/shard_map/context/pallas_call | solution.py:124
  48.3 10.8 %project.1 = (bf16[3,512,512]{2,1,0:T(8,128)(2,1)}, bf16[1024,512]{1,0:T(8,128)(2,1)}, bf16[2048,512]{1,0:T(8,128)(2,1)}, bf16[2048,512]{1,0:T(8,128)(2,1)}, bf1...) custom-call(s32[3]{0:T(128)} %pad_add_fusion.refs_0_.place_ref, bf16[2048,512]{1,0:T(8,128)(2,1)} %get-tuple-element.68.refs_1_, ...), custom_call_target="tpu_custom_call" | custom-call | flops 2684354560 | bytes 14000000 | tf_op jit(solution)/shard_map/project/pallas_call | solution.py:262
  59.8 37.1 %attend.1 = (bf16[8,2048,1024]{2,1,0:T(8,128)(2,1)}, f32[512,1024]{1,0:T(8,128)}, f32[512,1024]{1,0:T(8,128)}, f32[4,8,1024]{2,1,0:T(8,128)}, bf16[1024,512]{1,0:T(8,128)(2,1)}, /*index=5*/bf16[512,1024]{1,0:T(8,128)(2,1)}) custom-call(bf16[1024,512]{1,0:T(8,128)(2,1)} %get-tuple-element.69.q_ref, bf16[2048,512]{1,0:T(8,128)(2,1)} %get-tuple-element.70.k_ref, ...), custom_call_target="tpu_custom_call" | custom-call | flops 8589934592 | bytes 62000000 | tf_op jit(solution)/shard_map/attend/pallas_call | solution.py:334
  98.0 34.5 %feed.1 = (bf16[1024,512]{1,0:T(8,128)(2,1)}, bf16[1024,2048]{1,0:T(8,128)(2,1)}, bf16[1024,2048]{1,0:T(8,128)(2,1)}, bf16[512,1024]{1,0:T(8,128)(2,1)}, bf16[10...) custom-call(s32[3]{0:T(128)} %pad_add_fusion.refs_0_.place_ref, ...), custom_call_target="tpu_custom_call" | custom-call | flops 9663676416 | bytes 22000000 | tf_op jit(solution)/shard_map/feed/pallas_call | solution.py:464
  132.4 12.0 %feed_grads.1 = (bf16[4,4,64,1152]{3,2,1,0:T(8,128)(2,1)}, bf16[4,4,64,1152]{3,2,1,0:T(8,128)(2,1)}) custom-call(s32[3]{0:T(128)} %pad_add_fusion.refs_0_.place_ref, bf16[512,1024]{1,0:T(8,128)(2,1)} %get-tuple-element.94.cott_ref, bf16[1024,2048]{1,0:T(8,128)(2,1)} %get-tuple-element.95.act_ref, bf16[512,1024]{1,0:T(8,128)(2,1)} %get-tuple-element.96.ffnt_ref, ...), custom_call_target="tpu_custom_call" | custom-call | flops 4831838208 | bytes 17000000 | tf_op jit(solution)/shard_map/feed_grads/pallas_call | solution.py:525
  144.8 41.3 %unattend.1 = (bf16[1024,512]{1,0:T(8,128)(2,1)}, bf16[2048,512]{1,0:T(8,128)(2,1)}, bf16[2048,512]{1,0:T(8,128)(2,1)}, f32[4,2,1024]{2,1,0:T(2,128)}) custom-call(bf16[1024,512]{1,0:T(8,128)(2,1)} %get-tuple-element.69.q_ref, bf16[2048,512]{1,0:T(8,128)(2,1)} %get-tuple-element.70.k_ref, bf16[512,2048]{1,0:T(8,128)(2,1)} %get-tuple-element.77.kt_ref, ...), custom_call_target="tpu_custom_call" | custom-call | flops 17179869184 | bytes 56000000 | tf_op jit(solution)/shard_map/unattend/pallas_call | solution.py:600
  186.0 8.2 %proj_grads.1 = (bf16[4,4,3,64,128]{4,3,2,1,0:T(8,128)(2,1)}, bf16[4,4,3,64,128]{4,3,2,1,0:T(8,128)(2,1)}, f32[8,512]{1,0:T(8,128)}) custom-call(s32[3]{0:T(128)} %pad_add_fusion.refs_0_.place_ref, bf16[512,2048]{1,0:T(8,128)(2,1)} %get-tuple-element.91.xt_ref, bf16[1024,512]{1,0:T(8,128)(2,1)} %get-tuple-element.84.dq_ref, ...), custom_call_target="tpu_custom_call" | custom-call | flops 2684354560 | bytes 10000000 | tf_op jit(solution)/shard_map/proj_grads/pallas_call | solution.py:688
  194.3 9.8 %input.1 = (bf16[1024,512]{1,0:T(8,128)(2,1)}, f32[1,512]{1,0:T(1,128)}) custom-call(bf16[1024,512]{1,0:T(8,128)(2,1)} %get-tuple-element.84.dq_ref, bf16[2048,512]{1,0:T(8,128)(2,1)} %get-tuple-element.85.dk_ref, bf16[2048,512]{1,0:T(8,128)(2,1)} %get-tuple-element.86.dv_ref, f32[4,2,1024]{2,1,0:T(2,128)} %get-tuple-element.87.gl_ref, ...), custom_call_target="tpu_custom_call" | custom-call | flops 2147483648 | bytes 10000000 | tf_op jit(solution)/shard_map/input/pallas_call | solution.py:735
  204.9 1.5 collective-permute-start.22
  207.9 1.9 fusion.4
  210.5 1.5 collective-permute-start.29
  214.6 2.8 collective-permute-start.34
  217.5 2.5 collective-permute-start.35
  220.7 8.3 %collective-permute-done.28 = bf16[4,64,1152]{2,1,0:T(8,128)(2,1)S(1)} collective-permute-done((bf16[4,64,1152]{2,1,0:T(8,128)(2,1)S(1)}, bf16[4,64,1152]{2,1,0:T(8,128)(2,1)S(1)}, u32[]{:S(2)}, u32[]{:S(2)}) %collective-permute-start.28) | collective-permute-done | bytes 589856 | tf_op jit(solution)/shard_map/ppermute | solution.py:760
  230.5 1.7 collective-permute-start.24
  232.2 10.4 %collective-permute-done.30 = bf16[4,64,1152]{2,1,0:T(8,128)(2,1)S(1)} collective-permute-done((bf16[4,64,1152]{2,1,0:T(8,128)(2,1)S(1)}, bf16[4,64,1152]{2,1,0:T(8,128)(2,1)S(1)}, u32[]{:S(2)}, u32[]{:S(2)}) %collective-permute-start.30) | collective-permute-done | bytes 589856 | tf_op jit(solution)/shard_map/ppermute | solution.py:760
  246.3 2.6 collective-permute-start.26
  248.9 1.8 collective-permute-start.32
  250.7 2.6 collective-permute-start.33
  253.5 1.8 collective-permute-start.38
  255.2 1.9 collective-permute-done.31.refs_5_
  257.1 2.1 collective-permute-start.39
  259.2 4.5 %collective-permute-done.32.refs_6_ = bf16[64,1152]{1,0:T(8,128)(2,1)S(1)} collective-permute-done((bf16[64,1152]{1,0:T(8,128)(2,1)S(1)}, bf16[64,1152]{1,0:T(8,128)(2,1)S(1)}, u32[]{:S(2)}, u32[]{:S(2)}) %collective-permute-start.32) | collective-permute-done | bytes 147488 | tf_op jit(solution)/shard_map/ppermute | solution.py:760
  264.4 2.2 owned.1
  266.6 5.4 %all-to-all-start = ((f32[32,8,128]{2,1,0:T(8,128)}), f32[32,8,128]{2,1,0:T(8,128)S(1)}, u32[]{:S(2)}, u32[]{:S(2)}) async-start(f32[32,8,128]{2,1,0:T(8,128)} %get-tuple-element.102), calls=%async_computation | async-start | bytes 262144 | tf_op jit(solution)/shard_map/all_to_all | solution.py:1109
  273.3 7.1 %all-to-all-done.sq_ref = f32[32,8,128]{2,1,0:T(8,128)S(1)} async-done(((f32[32,8,128]{2,1,0:T(8,128)}), f32[32,8,128]{2,1,0:T(8,128)S(1)}, u32[]{:S(2)}, u32[]{:S(2)}) %all-to-all-start) | async-done | bytes 131104 | tf_op jit(solution)/shard_map/all_to_all | solution.py:1109
  281.1 2.5 moment.1
  283.6 1.8 collective-permute-start.42
  285.4 2.6 collective-permute-start.43
  288.6 3.5 %collective-permute-done.42 = bf16[64,512]{1,0:T(8,128)(2,1)S(1)} collective-permute-done((bf16[64,512]{1,0:T(8,128)(2,1)}, bf16[64,512]{1,0:T(8,128)(2,1)S(1)}, u32[]{:S(2)}, u32[]{:S(2)}) %collective-permute-start.42) | collective-permute-done | bytes 65568 | tf_op jit(solution)/shard_map/ppermute | solution.py:760
  294.5 2.1 collective-permute-start.46
  296.6 5.1 %collective-permute-done.44.refs_1_ = bf16[4,64,512]{2,1,0:T(8,128)(2,1)S(1)} collective-permute-done((bf16[4,64,512]{2,1,0:T(8,128)(2,1)S(1)}, bf16[4,64,512]{2,1,0:T(8,128)(2,1)S(1)}, u32[]{:S(2)}, u32[]{:S(2)}) %collective-permute-start.44) | collective-permute-done | bytes 262176 | tf_op jit(solution)/shard_map/ppermute | solution.py:760
  301.7 3.5 %collective-permute-done.45.refs_2_ = bf16[4,64,512]{2,1,0:T(8,128)(2,1)S(1)} collective-permute-done((bf16[4,64,512]{2,1,0:T(8,128)(2,1)S(1)}, bf16[4,64,512]{2,1,0:T(8,128)(2,1)S(1)}, u32[]{:S(2)}, u32[]{:S(2)}) %collective-permute-start.45) | collective-permute-done | bytes 262176 | tf_op jit(solution)/shard_map/ppermute | solution.py:760
  308.2 15.4 %orthogonal.1 = (bf16[64,512]{1,0:T(8,128)(2,1)}, bf16[64,512]{1,0:T(8,128)(2,1)}, bf16[64,512]{1,0:T(8,128)(2,1)}, bf16[64,512]{1,0:T(8,128)(2,1)}) custom-call(s32[3]{0:T(128)} %pad_add_fusion.refs_0_.place_ref, bf16[4,64,512]{2,1,0:T(8,128)(2,1)} %copy-done.6, bf16[4,64,512]{2,1,0:T(8,128)(2,1)} %copy-done.29, bf16[4,64,512]{2,1,0:T(8,128)(2,1)} %copy-done.30, ...), custom_call_target="tpu_custom_call" | custom-call | flops 12000000000 | bytes 3000000 | tf_op jit(solution)/shard_map/orthogonal/pallas_call | solution.py:938
  323.5 1.6 collective-permute-start.51
  326.4 1.6 collective-permute-start.53
  329.5 3.6 %collective-permute-done.52.refs_2_ = bf16[64,512]{1,0:T(8,128)(2,1)S(1)} collective-permute-done((bf16[64,512]{1,0:T(8,128)(2,1)}, bf16[64,512]{1,0:T(8,128)(2,1)S(1)}, u32[]{:S(2)}, u32[]{:S(2)}) %collective-permute-start.52) | collective-permute-done | bytes 65568 | tf_op jit(solution)/shard_map/ppermute | solution.py:760
  333.8 2.1 update.1
  335.9 1.7 copy.32
  (184 shorter events, 39.4 us)
Async XLA Ops:
  1.6 7.5 %collective-permute-start = (bf16[3,64,128]{2,1,0:T(8,128)(2,1)S(1)}, bf16[3,64,128]{2,1,0:T(8,128)(2,1)S(1)}, u32[]{:S(2)}, u32[]{:S(2)}) collective-permute-start(bf16[3,64,128]{2,1,0:T(8,128)(2,1)S(1)} %get-tuple-element.164), channel_id=1, source_target_pairs={{0,1},{1,0},{2,3},{3,2},{4,5},{5,4},{6,7},{7,6},{8,9},{9,8},{10,11... | collective-permute-start | bytes 147464 | tf_op jit(solution)/shard_map/ppermute | solution.py:760
  4.7 5.9 %collective-permute-start.1 = (bf16[3,64,128]{2,1,0:T(8,128)(2,1)S(1)}, bf16[3,64,128]{2,1,0:T(8,128)(2,1)S(1)}, u32[]{:S(2)}, u32[]{:S(2)}) collective-permute-start(bf16[3,64,128]{2,1,0:T(8,128)(2,1)S(1)} %get-tuple-element.164), channel_id=1, source_target_pairs={{0,2},{1,3},{2,0},{3,1},{4,6},{5,7},{6,4},{7,5},{8,10},{9,11},{10,... | collective-permute-start | bytes 147464 | tf_op jit(solution)/shard_map/ppermute | solution.py:760
  7.3 5.9 %collective-permute-start.2 = (bf16[3,64,128]{2,1,0:T(8,128)(2,1)S(1)}, bf16[3,64,128]{2,1,0:T(8,128)(2,1)S(1)}, u32[]{:S(2)}, u32[]{:S(2)}) collective-permute-start(bf16[3,64,128]{2,1,0:T(8,128)(2,1)S(1)} %get-tuple-element.164), channel_id=1, source_target_pairs={{0,3},{1,2},{2,1},{3,0},{4,7},{5,6},{6,5},{7,4},{8,11},{9,10},{10,... | collective-permute-start | bytes 147464 | tf_op jit(solution)/shard_map/ppermute | solution.py:760
  13.2 14.3 %collective-permute-start.3 = (bf16[4,3,64,128]{3,2,1,0:T(8,128)(2,1)S(1)}, bf16[4,3,64,128]{3,2,1,0:T(8,128)(2,1)S(1)}, u32[]{:S(2)}, u32[]{:S(2)}) collective-permute-start(bf16[4,3,64,128]{3,2,1,0:T(8,128)(2,1)S(1)} %pad_maximum_fusion.2.refs_2_), channel_id=1, source_target_pairs={{0,8},{8,0},{16,24},{24,16},{1,9},{9,1},{17,25},{25,17},{2,10},{10... | collective-permute-start | bytes 589832 | tf_op jit(solution)/shard_map/ppermute | solution.py:760
  14.8 7.2 %collective-permute-start.10 = (bf16[64,1152]{1,0:T(8,128)(2,1)S(1)}, bf16[64,1152]{1,0:T(8,128)(2,1)S(1)}, u32[]{:S(2)}, u32[]{:S(2)}) collective-permute-start(bf16[64,1152]{1,0:T(8,128)(2,1)S(1)} %get-tuple-element.162), channel_id=1, source_target_pairs={{0,1},{1,0},{2,3},{3,2},{4,5},{5,4},{6,7},{7,6},{8,9},{9,8},{10,11... | collective-permute-start | bytes 442376 | tf_op jit(solution)/shard_map/ppermute | solution.py:760
  14.9 12.6 %collective-permute-start.11 = (bf16[64,1152]{1,0:T(8,128)(2,1)S(1)}, bf16[64,1152]{1,0:T(8,128)(2,1)S(1)}, u32[]{:S(2)}, u32[]{:S(2)}) collective-permute-start(bf16[64,1152]{1,0:T(8,128)(2,1)S(1)} %get-tuple-element.162), channel_id=1, source_target_pairs={{0,2},{1,3},{2,0},{3,1},{4,6},{5,7},{6,4},{7,5},{8,10},{9,11},{10,... | collective-permute-start | bytes 442376 | tf_op jit(solution)/shard_map/ppermute | solution.py:760
  16.1 11.9 %collective-permute-start.12 = (bf16[64,1152]{1,0:T(8,128)(2,1)S(1)}, bf16[64,1152]{1,0:T(8,128)(2,1)S(1)}, u32[]{:S(2)}, u32[]{:S(2)}) collective-permute-start(bf16[64,1152]{1,0:T(8,128)(2,1)S(1)} %get-tuple-element.162), channel_id=1, source_target_pairs={{0,3},{1,2},{2,1},{3,0},{4,7},{5,6},{6,5},{7,4},{8,11},{9,10},{10,... | collective-permute-start | bytes 442376 | tf_op jit(solution)/shard_map/ppermute | solution.py:760
  20.4 8.3 %collective-permute-start.4 = (bf16[4,3,64,128]{3,2,1,0:T(8,128)(2,1)S(1)}, bf16[4,3,64,128]{3,2,1,0:T(8,128)(2,1)S(1)}, u32[]{:S(2)}, u32[]{:S(2)}) collective-permute-start(bf16[4,3,64,128]{3,2,1,0:T(8,128)(2,1)S(1)} %pad_maximum_fusion.2.refs_2_), channel_id=1, source_target_pairs={{0,16},{8,24},{16,0},{24,8},{1,17},{9,25},{17,1},{25,9},{2,18},{10... | collective-permute-start | bytes 589832 | tf_op jit(solution)/shard_map/ppermute | solution.py:760
  22.0 8.2 %collective-permute-start.5 = (bf16[4,3,64,128]{3,2,1,0:T(8,128)(2,1)S(1)}, bf16[4,3,64,128]{3,2,1,0:T(8,128)(2,1)}, u32[]{:S(2)}, u32[]{:S(2)}) collective-permute-start(bf16[4,3,64,128]{3,2,1,0:T(8,128)(2,1)S(1)} %pad_maximum_fusion.2.refs_2_), channel_id=1, source_target_pairs={{0,24},{8,16},{16,8},{24,0},{1,25},{9,17},{17,9},{25,1},{2,26},{10... | collective-permute-start | bytes 589832 | tf_op jit(solution)/shard_map/ppermute | solution.py:760
  28.1 31.0 %collective-permute-start.13 = (bf16[4,64,1152]{2,1,0:T(8,128)(2,1)S(1)}, bf16[4,64,1152]{2,1,0:T(8,128)(2,1)S(1)}, u32[]{:S(2)}, u32[]{:S(2)}) collective-permute-start(bf16[4,64,1152]{2,1,0:T(8,128)(2,1)S(1)} %pad_maximum_fusion.refs_5_), channel_id=1, source_target_pairs={{0,8},{8,0},{16,24},{24,16},{1,9},{9,1},{17,25},{25,17},{2,10},{10... | collective-permute-start | bytes 1769480 | tf_op jit(solution)/shard_map/ppermute | solution.py:760
  28.7 30.5 %collective-permute-start.14 = (bf16[4,64,1152]{2,1,0:T(8,128)(2,1)S(1)}, bf16[4,64,1152]{2,1,0:T(8,128)(2,1)S(1)}, u32[]{:S(2)}, u32[]{:S(2)}) collective-permute-start(bf16[4,64,1152]{2,1,0:T(8,128)(2,1)S(1)} %pad_maximum_fusion.refs_5_), channel_id=1, source_target_pairs={{0,16},{8,24},{16,0},{24,8},{1,17},{9,25},{17,1},{25,9},{2,18},{10... | collective-permute-start | bytes 1769480 | tf_op jit(solution)/shard_map/ppermute | solution.py:760
  30.2 29.5 %collective-permute-start.15 = (bf16[4,64,1152]{2,1,0:T(8,128)(2,1)S(1)}, bf16[4,64,1152]{2,1,0:T(8,128)(2,1)S(1)}, u32[]{:S(2)}, u32[]{:S(2)}) collective-permute-start(bf16[4,64,1152]{2,1,0:T(8,128)(2,1)S(1)} %pad_maximum_fusion.refs_5_), channel_id=1, source_target_pairs={{0,24},{8,16},{16,8},{24,0},{1,25},{9,17},{17,9},{25,1},{2,26},{10... | collective-permute-start | bytes 1769480 | tf_op jit(solution)/shard_map/ppermute | solution.py:760
  31.7 16.2 %collective-permute-start.8 = (bf16[4,3,64,128]{3,2,1,0:T(8,128)(2,1)S(1)}, bf16[4,3,64,128]{3,2,1,0:T(8,128)(2,1)}, u32[]{:S(2)}, u32[]{:S(2)}) collective-permute-start(bf16[4,3,64,128]{3,2,1,0:T(8,128)(2,1)S(1)} %collective-permute-done.4.refs_4_), channel_id=1, source_target_pairs={{0,4},{4,0},{1,5},{5,1},{2,6},{6,2},{3,7},{7,3},{8,12},{12,8},{9,1... | collective-permute-start | bytes 589832 | tf_op jit(solution)/shard_map/ppermute | solution.py:760
  31.7 16.6 %collective-permute-start.9 = (bf16[4,3,64,128]{3,2,1,0:T(8,128)(2,1)}, bf16[4,3,64,128]{3,2,1,0:T(8,128)(2,1)}, u32[]{:S(2)}, u32[]{:S(2)}) collective-permute-start(bf16[4,3,64,128]{3,2,1,0:T(8,128)(2,1)} %collective-permute-done.5.refs_5_), channel_id=1, source_target_pairs={{0,4},{4,0},{1,5},{5,1},{2,6},{6,2},{3,7},{7,3},{8,12},{12,8},{9,1... | collective-permute-start | bytes 589832 | tf_op jit(solution)/shard_map/ppermute | solution.py:760
  47.8 49.1 %collective-permute-start.16 = (bf16[4,64,1152]{2,1,0:T(8,128)(2,1)S(1)}, bf16[4,64,1152]{2,1,0:T(8,128)(2,1)S(1)}, u32[]{:S(2)}, u32[]{:S(2)}) collective-permute-start(bf16[4,64,1152]{2,1,0:T(8,128)(2,1)S(1)} %pad_maximum_fusion.refs_5_), channel_id=1, source_target_pairs={{0,4},{4,0},{1,5},{5,1},{2,6},{6,2},{3,7},{7,3},{8,12},{12,8},{9,1... | collective-permute-start | bytes 1769480 | tf_op jit(solution)/shard_map/ppermute | solution.py:760
  59.1 37.8 %collective-permute-start.17 = (bf16[4,64,1152]{2,1,0:T(8,128)(2,1)S(1)}, bf16[4,64,1152]{2,1,0:T(8,128)(2,1)S(1)}, u32[]{:S(2)}, u32[]{:S(2)}) collective-permute-start(bf16[4,64,1152]{2,1,0:T(8,128)(2,1)S(1)} %collective-permute-done.13.refs_6_), channel_id=1, source_target_pairs={{0,4},{4,0},{1,5},{5,1},{2,6},{6,2},{3,7},{7,3},{8,12},{12,8},{9,1... | collective-permute-start | bytes 1769480 | tf_op jit(solution)/shard_map/ppermute | solution.py:760
  59.3 37.7 %collective-permute-start.18 = (bf16[4,64,1152]{2,1,0:T(8,128)(2,1)S(1)}, bf16[4,64,1152]{2,1,0:T(8,128)(2,1)}, u32[]{:S(2)}, u32[]{:S(2)}) collective-permute-start(bf16[4,64,1152]{2,1,0:T(8,128)(2,1)S(1)} %collective-permute-done.14.refs_7_), channel_id=1, source_target_pairs={{0,4},{4,0},{1,5},{5,1},{2,6},{6,2},{3,7},{7,3},{8,12},{12,8},{9,1... | collective-permute-start | bytes 1769480 | tf_op jit(solution)/shard_map/ppermute | solution.py:760
  59.7 37.3 %collective-permute-start.19 = (bf16[4,64,1152]{2,1,0:T(8,128)(2,1)S(1)}, bf16[4,64,1152]{2,1,0:T(8,128)(2,1)}, u32[]{:S(2)}, u32[]{:S(2)}) collective-permute-start(bf16[4,64,1152]{2,1,0:T(8,128)(2,1)S(1)} %collective-permute-done.15.refs_8_), channel_id=1, source_target_pairs={{0,4},{4,0},{1,5},{5,1},{2,6},{6,2},{3,7},{7,3},{8,12},{12,8},{9,1... | collective-permute-start | bytes 1769480 | tf_op jit(solution)/shard_map/ppermute | solution.py:760
  144.4 63.5 %collective-permute-start.27 = (bf16[4,4,64,1152]{3,2,1,0:T(8,128)(2,1)}, bf16[4,4,64,1152]{3,2,1,0:T(8,128)(2,1)}, u32[]{:S(2)}, u32[]{:S(2)}) collective-permute-start(bf16[4,4,64,1152]{3,2,1,0:T(8,128)(2,1)} %get-tuple-element.101), channel_id=1, source_target_pairs={{0,4},{4,0},{1,5},{5,1},{2,6},{6,2},{3,7},{7,3},{8,12},{12,8},{9,1... | collective-permute-start | bytes 7077896 | tf_op jit(solution)/shard_map/ppermute | solution.py:760
  194.2 9.9 %collective-permute-start.20 = (bf16[4,4,3,64,128]{4,3,2,1,0:T(8,128)(2,1)}, bf16[4,4,3,64,128]{4,3,2,1,0:T(8,128)(2,1)S(1)}, u32[]{:S(2)}, u32[]{:S(2)}) collective-permute-start(bf16[4,4,3,64,128]{4,3,2,1,0:T(8,128)(2,1)} %get-tuple-element.93), channel_id=1, source_target_pairs={{0,4},{4,0},{1,5},{5,1},{2,6},{6,2},{3,7},{7,3},{8,12},{12,8},{9,1... | collective-permute-start | bytes 2359304 | tf_op jit(solution)/shard_map/ppermute | solution.py:760
  204.3 7.8 %collective-permute-start.21 = (bf16[4,3,64,128]{3,2,1,0:T(8,128)(2,1)S(1)}, bf16[4,3,64,128]{3,2,1,0:T(8,128)(2,1)S(1)}, u32[]{:S(2)}, u32[]{:S(2)}) collective-permute-start(bf16[4,3,64,128]{3,2,1,0:T(8,128)(2,1)S(1)} %get-tuple-element.150), channel_id=1, source_target_pairs={{0,8},{8,0},{16,24},{24,16},{1,9},{9,1},{17,25},{25,17},{2,10},{10... | collective-permute-start | bytes 589832 | tf_op jit(solution)/shard_map/ppermute | solution.py:760
  204.9 9.7 %collective-permute-start.22 = (bf16[4,3,64,128]{3,2,1,0:T(8,128)(2,1)S(1)}, bf16[4,3,64,128]{3,2,1,0:T(8,128)(2,1)S(1)}, u32[]{:S(2)}, u32[]{:S(2)}) collective-permute-start(bf16[4,3,64,128]{3,2,1,0:T(8,128)(2,1)S(1)} %get-tuple-element.152), channel_id=1, source_target_pairs={{0,16},{8,24},{16,0},{24,8},{1,17},{9,25},{17,1},{25,9},{2,18},{10... | collective-permute-start | bytes 589832 | tf_op jit(solution)/shard_map/ppermute | solution.py:760
  206.5 11.0 %collective-permute-start.23 = (bf16[4,3,64,128]{3,2,1,0:T(8,128)(2,1)S(1)}, bf16[4,3,64,128]{3,2,1,0:T(8,128)(2,1)S(1)}, u32[]{:S(2)}, u32[]{:S(2)}) collective-permute-start(bf16[4,3,64,128]{3,2,1,0:T(8,128)(2,1)S(1)} %get-tuple-element.151), channel_id=1, source_target_pairs={{0,24},{8,16},{16,8},{24,0},{1,25},{9,17},{17,9},{25,1},{2,26},{10... | collective-permute-start | bytes 589832 | tf_op jit(solution)/shard_map/ppermute | solution.py:760
  209.9 19.2 %collective-permute-start.28 = (bf16[4,64,1152]{2,1,0:T(8,128)(2,1)S(1)}, bf16[4,64,1152]{2,1,0:T(8,128)(2,1)S(1)}, u32[]{:S(2)}, u32[]{:S(2)}) collective-permute-start(bf16[4,64,1152]{2,1,0:T(8,128)(2,1)S(1)} %get-tuple-element.147), channel_id=1, source_target_pairs={{0,8},{8,0},{16,24},{24,16},{1,9},{9,1},{17,25},{25,17},{2,10},{10... | collective-permute-start | bytes 1769480 | tf_op jit(solution)/shard_map/ppermute | solution.py:760
  210.5 20.1 %collective-permute-start.29 = (bf16[4,64,1152]{2,1,0:T(8,128)(2,1)S(1)}, bf16[4,64,1152]{2,1,0:T(8,128)(2,1)S(1)}, u32[]{:S(2)}, u32[]{:S(2)}) collective-permute-start(bf16[4,64,1152]{2,1,0:T(8,128)(2,1)S(1)} %get-tuple-element.149), channel_id=1, source_target_pairs={{0,16},{8,24},{16,0},{24,8},{1,17},{9,25},{17,1},{25,9},{2,18},{10... | collective-permute-start | bytes 1769480 | tf_op jit(solution)/shard_map/ppermute | solution.py:760
  212.1 30.5 %collective-permute-start.30 = (bf16[4,64,1152]{2,1,0:T(8,128)(2,1)S(1)}, bf16[4,64,1152]{2,1,0:T(8,128)(2,1)S(1)}, u32[]{:S(2)}, u32[]{:S(2)}) collective-permute-start(bf16[4,64,1152]{2,1,0:T(8,128)(2,1)S(1)} %get-tuple-element.148), channel_id=1, source_target_pairs={{0,24},{8,16},{16,8},{24,0},{1,25},{9,17},{17,9},{25,1},{2,26},{10... | collective-permute-start | bytes 1769480 | tf_op jit(solution)/shard_map/ppermute | solution.py:760
  214.6 31.7 %collective-permute-start.34 = (f32[10,512]{1,0:T(8,128)S(1)}, f32[10,512]{1,0:T(8,128)S(1)}, u32[]{:S(2)}, u32[]{:S(2)}) collective-permute-start(f32[10,512]{1,0:T(8,128)S(1)} %pad_maximum_fusion.4), channel_id=1, source_target_pairs={{0,8},{8,0},{16,24},{24,16},{1,9},{9,1},{17,25},{25,17},{2,10},{10... | collective-permute-start | bytes 61448 | tf_op jit(solution)/shard_map/ppermute | solution.py:760
  217.5 31.5 %collective-permute-start.35 = (f32[10,512]{1,0:T(8,128)S(1)}, f32[10,512]{1,0:T(8,128)S(1)}, u32[]{:S(2)}, u32[]{:S(2)}) collective-permute-start(f32[10,512]{1,0:T(8,128)S(1)} %pad_maximum_fusion.4), channel_id=1, source_target_pairs={{0,16},{8,24},{16,0},{24,8},{1,17},{9,25},{17,1},{25,9},{2,18},{10... | collective-permute-start | bytes 61448 | tf_op jit(solution)/shard_map/ppermute | solution.py:760
  229.0 19.9 %collective-permute-start.36 = (f32[10,512]{1,0:T(8,128)S(1)}, f32[10,512]{1,0:T(8,128)S(1)}, u32[]{:S(2)}, u32[]{:S(2)}) collective-permute-start(f32[10,512]{1,0:T(8,128)S(1)} %pad_maximum_fusion.4), channel_id=1, source_target_pairs={{0,24},{8,16},{16,8},{24,0},{1,25},{9,17},{17,9},{25,1},{2,26},{10... | collective-permute-start | bytes 61448 | tf_op jit(solution)/shard_map/ppermute | solution.py:760
  230.5 20.2 %collective-permute-start.24 = (bf16[3,64,128]{2,1,0:T(8,128)(2,1)S(1)}, bf16[3,64,128]{2,1,0:T(8,128)(2,1)S(1)}, u32[]{:S(2)}, u32[]{:S(2)}) collective-permute-start(bf16[3,64,128]{2,1,0:T(8,128)(2,1)S(1)} %get-tuple-element.159), channel_id=1, source_target_pairs={{0,1},{1,0},{2,3},{3,2},{4,5},{5,4},{6,7},{7,6},{8,9},{9,8},{10,11... | collective-permute-start | bytes 147464 | tf_op jit(solution)/shard_map/ppermute | solution.py:760
  242.7 10.7 %collective-permute-start.25 = (bf16[3,64,128]{2,1,0:T(8,128)(2,1)S(1)}, bf16[3,64,128]{2,1,0:T(8,128)(2,1)S(1)}, u32[]{:S(2)}, u32[]{:S(2)}) collective-permute-start(bf16[3,64,128]{2,1,0:T(8,128)(2,1)S(1)} %get-tuple-element.158), channel_id=1, source_target_pairs={{0,2},{1,3},{2,0},{3,1},{4,6},{5,7},{6,4},{7,5},{8,10},{9,11},{10,... | collective-permute-start | bytes 147464 | tf_op jit(solution)/shard_map/ppermute | solution.py:760
  246.3 7.1 %collective-permute-start.26 = (bf16[3,64,128]{2,1,0:T(8,128)(2,1)S(1)}, bf16[3,64,128]{2,1,0:T(8,128)(2,1)S(1)}, u32[]{:S(2)}, u32[]{:S(2)}) collective-permute-start(bf16[3,64,128]{2,1,0:T(8,128)(2,1)S(1)} %get-tuple-element.157), channel_id=1, source_target_pairs={{0,3},{1,2},{2,1},{3,0},{4,7},{5,6},{6,5},{7,4},{8,11},{9,10},{10,... | collective-permute-start | bytes 147464 | tf_op jit(solution)/shard_map/ppermute | solution.py:760
  248.9 8.2 %collective-permute-start.31 = (bf16[64,1152]{1,0:T(8,128)(2,1)S(1)}, bf16[64,1152]{1,0:T(8,128)(2,1)S(1)}, u32[]{:S(2)}, u32[]{:S(2)}) collective-permute-start(bf16[64,1152]{1,0:T(8,128)(2,1)S(1)} %get-tuple-element.155), channel_id=1, source_target_pairs={{0,1},{1,0},{2,3},{3,2},{4,5},{5,4},{6,7},{7,6},{8,9},{9,8},{10,11... | collective-permute-start | bytes 442376 | tf_op jit(solution)/shard_map/ppermute | solution.py:760
  248.9 14.7 %collective-permute-start.32 = (bf16[64,1152]{1,0:T(8,128)(2,1)S(1)}, bf16[64,1152]{1,0:T(8,128)(2,1)S(1)}, u32[]{:S(2)}, u32[]{:S(2)}) collective-permute-start(bf16[64,1152]{1,0:T(8,128)(2,1)S(1)} %get-tuple-element.154), channel_id=1, source_target_pairs={{0,2},{1,3},{2,0},{3,1},{4,6},{5,7},{6,4},{7,5},{8,10},{9,11},{10,... | collective-permute-start | bytes 442376 | tf_op jit(solution)/shard_map/ppermute | solution.py:760
  250.7 12.9 %collective-permute-start.33 = (bf16[64,1152]{1,0:T(8,128)(2,1)S(1)}, bf16[64,1152]{1,0:T(8,128)(2,1)S(1)}, u32[]{:S(2)}, u32[]{:S(2)}) collective-permute-start(bf16[64,1152]{1,0:T(8,128)(2,1)S(1)} %get-tuple-element.153), channel_id=1, source_target_pairs={{0,3},{1,2},{2,1},{3,0},{4,7},{5,6},{6,5},{7,4},{8,11},{9,10},{10,... | collective-permute-start | bytes 442376 | tf_op jit(solution)/shard_map/ppermute | solution.py:760
  253.4 18.6 %collective-permute-start.37 = (f32[10,512]{1,0:T(8,128)S(1)}, f32[10,512]{1,0:T(8,128)S(1)}, u32[]{:S(2)}, u32[]{:S(2)}) collective-permute-start(f32[10,512]{1,0:T(8,128)S(1)} %add_add_fusion.1), channel_id=1, source_target_pairs={{0,1},{1,0},{2,3},{3,2},{4,5},{5,4},{6,7},{7,6},{8,9},{9,8},{10,11... | collective-permute-start | bytes 61448 | tf_op jit(solution)/shard_map/ppermute | solution.py:760
  253.5 18.6 %collective-permute-start.38 = (f32[10,512]{1,0:T(8,128)S(1)}, f32[10,512]{1,0:T(8,128)S(1)}, u32[]{:S(2)}, u32[]{:S(2)}) collective-permute-start(f32[10,512]{1,0:T(8,128)S(1)} %add_add_fusion.1), channel_id=1, source_target_pairs={{0,2},{1,3},{2,0},{3,1},{4,6},{5,7},{6,4},{7,5},{8,10},{9,11},{10,... | collective-permute-start | bytes 61448 | tf_op jit(solution)/shard_map/ppermute | solution.py:760
  257.1 14.9 %collective-permute-start.39 = (f32[10,512]{1,0:T(8,128)S(1)}, f32[10,512]{1,0:T(8,128)S(1)}, u32[]{:S(2)}, u32[]{:S(2)}) collective-permute-start(f32[10,512]{1,0:T(8,128)S(1)} %add_add_fusion.1), channel_id=1, source_target_pairs={{0,3},{1,2},{2,1},{3,0},{4,7},{5,6},{6,5},{7,4},{8,11},{9,10},{10,... | collective-permute-start | bytes 61448 | tf_op jit(solution)/shard_map/ppermute | solution.py:760
  266.6 13.8 %all-to-all-start = ((f32[32,8,128]{2,1,0:T(8,128)}), f32[32,8,128]{2,1,0:T(8,128)S(1)}, u32[]{:S(2)}, u32[]{:S(2)}) async-start(f32[32,8,128]{2,1,0:T(8,128)} %get-tuple-element.102), calls=%async_computation | async-start | bytes 262144 | tf_op jit(solution)/shard_map/all_to_all | solution.py:1109
  283.6 8.5 %collective-permute-start.42 = (bf16[64,512]{1,0:T(8,128)(2,1)}, bf16[64,512]{1,0:T(8,128)(2,1)S(1)}, u32[]{:S(2)}, u32[]{:S(2)}) collective-permute-start(bf16[64,512]{1,0:T(8,128)(2,1)} %get-tuple-element.110), channel_id=1, source_target_pairs={{0,2},{1,3},{2,0},{3,1},{4,6},{5,7},{6,4},{7,5},{8,10},{9,11},{10,... | collective-permute-start | bytes 196616 | tf_op jit(solution)/shard_map/ppermute | solution.py:760
  285.4 6.7 %collective-permute-start.43 = (bf16[64,512]{1,0:T(8,128)(2,1)}, bf16[64,512]{1,0:T(8,128)(2,1)S(1)}, u32[]{:S(2)}, u32[]{:S(2)}) collective-permute-start(bf16[64,512]{1,0:T(8,128)(2,1)} %get-tuple-element.111), channel_id=1, source_target_pairs={{0,3},{1,2},{2,1},{3,0},{4,7},{5,6},{6,5},{7,4},{8,11},{9,10},{10,... | collective-permute-start | bytes 196616 | tf_op jit(solution)/shard_map/ppermute | solution.py:760
  293.0 8.7 %collective-permute-start.44 = (bf16[4,64,512]{2,1,0:T(8,128)(2,1)S(1)}, bf16[4,64,512]{2,1,0:T(8,128)(2,1)S(1)}, u32[]{:S(2)}, u32[]{:S(2)}) collective-permute-start(bf16[4,64,512]{2,1,0:T(8,128)(2,1)S(1)} %pad_maximum_fusion.1.refs_0_), channel_id=1, source_target_pairs={{0,8},{8,0},{16,24},{24,16},{1,9},{9,1},{17,25},{25,17},{2,10},{10... | collective-permute-start | bytes 786440 | tf_op jit(solution)/shard_map/ppermute | solution.py:760
  293.8 11.3 %collective-permute-start.45 = (bf16[4,64,512]{2,1,0:T(8,128)(2,1)S(1)}, bf16[4,64,512]{2,1,0:T(8,128)(2,1)S(1)}, u32[]{:S(2)}, u32[]{:S(2)}) collective-permute-start(bf16[4,64,512]{2,1,0:T(8,128)(2,1)S(1)} %pad_maximum_fusion.1.refs_0_), channel_id=1, source_target_pairs={{0,16},{8,24},{16,0},{24,8},{1,17},{9,25},{17,1},{25,9},{2,18},{10... | collective-permute-start | bytes 786440 | tf_op jit(solution)/shard_map/ppermute | solution.py:760
  294.5 10.7 %collective-permute-start.46 = (bf16[4,64,512]{2,1,0:T(8,128)(2,1)S(1)}, bf16[4,64,512]{2,1,0:T(8,128)(2,1)S(1)}, u32[]{:S(2)}, u32[]{:S(2)}) collective-permute-start(bf16[4,64,512]{2,1,0:T(8,128)(2,1)S(1)} %pad_maximum_fusion.1.refs_0_), channel_id=1, source_target_pairs={{0,24},{8,16},{16,8},{24,0},{1,25},{9,17},{17,9},{25,1},{2,26},{10... | collective-permute-start | bytes 786440 | tf_op jit(solution)/shard_map/ppermute | solution.py:760
  296.6 9.1 %collective-permute-start.47 = (bf16[4,64,512]{2,1,0:T(8,128)(2,1)S(1)}, bf16[4,64,512]{2,1,0:T(8,128)(2,1)S(1)}, u32[]{:S(2)}, u32[]{:S(2)}) collective-permute-start(bf16[4,64,512]{2,1,0:T(8,128)(2,1)S(1)} %pad_maximum_fusion.1.refs_0_), channel_id=1, source_target_pairs={{0,4},{4,0},{1,5},{5,1},{2,6},{6,2},{3,7},{7,3},{8,12},{12,8},{9,1... | collective-permute-start | bytes 786440 | tf_op jit(solution)/shard_map/ppermute | solution.py:760
  323.5 6.0 %collective-permute-start.51 = (bf16[64,512]{1,0:T(8,128)(2,1)}, bf16[64,512]{1,0:T(8,128)(2,1)S(1)}, u32[]{:S(2)}, u32[]{:S(2)}) collective-permute-start(bf16[64,512]{1,0:T(8,128)(2,1)} %get-tuple-element.113), channel_id=1, source_target_pairs={{0,1},{1,0},{2,3},{3,2},{4,5},{5,4},{6,7},{7,6},{8,9},{9,8},{10,11... | collective-permute-start | bytes 196616 | tf_op jit(solution)/shard_map/ppermute | solution.py:760
  325.2 8.0 %collective-permute-start.52 = (bf16[64,512]{1,0:T(8,128)(2,1)}, bf16[64,512]{1,0:T(8,128)(2,1)S(1)}, u32[]{:S(2)}, u32[]{:S(2)}) collective-permute-start(bf16[64,512]{1,0:T(8,128)(2,1)} %get-tuple-element.114), channel_id=1, source_target_pairs={{0,2},{1,3},{2,0},{3,1},{4,6},{5,7},{6,4},{7,5},{8,10},{9,11},{10,... | collective-permute-start | bytes 196616 | tf_op jit(solution)/shard_map/ppermute | solution.py:760
  326.4 6.8 %collective-permute-start.53 = (bf16[64,512]{1,0:T(8,128)(2,1)}, bf16[64,512]{1,0:T(8,128)(2,1)S(1)}, u32[]{:S(2)}, u32[]{:S(2)}) collective-permute-start(bf16[64,512]{1,0:T(8,128)(2,1)} %get-tuple-element.115), channel_id=1, source_target_pairs={{0,3},{1,2},{2,1},{3,0},{4,7},{5,6},{6,5},{7,4},{8,11},{9,10},{10,... | collective-permute-start | bytes 196616 | tf_op jit(solution)/shard_map/ppermute | solution.py:760
  (47 other events, 460.2 us)
